TPU v7x, 32 devices: a whole 2x2x4 slice. The times are simulated.
32 devices in a mesh: rows: 8 (over z, x), seq: 4 (over y, core).
Axes of the slice: x: 2, y: 2, z: 4, core: 2. Of those that a mesh axis runs over, the one named last changes fastest.
Arguments:
- layer_input: float32 [8, 1024, 768], P('rows', 'seq'), may hold values from -6 to 6
- doc_lengths: int32 [8, 4], P('rows'), may hold values from 1 to 976, as said below
- output_grad: float32 [8, 1024, 768], P('rows', 'seq'), may hold values from -6 to 6
- mixer_gain: float32 [768], replicated, may hold values from 0.5 to 1.5
- triple_weight: float32 [768, 2304], replicated, may hold values from -0.21875 to 0.21875
- rate_weight: float32 [768, 12], replicated, may hold values from -0.21875 to 0.21875
- rate_bias: float32 [12], replicated, may hold values from -3 to 3
- first_weight: float32 [12, 64, 256], replicated, may hold values from -0.75 to 0.75
- first_bias: float32 [12, 256], replicated, may hold values from -3 to 3
- second_weight: float32 [12, 256, 64], replicated, may hold values from -0.375 to 0.375
- second_bias: float32 [12, 64], replicated, may hold values from -3 to 3
- inner_gain: float32 [12, 64], replicated, may hold values from 0.5 to 1.5
- inner_shift: float32 [12, 64], replicated, may hold values from -3 to 3
- gate_weight: float32 [768, 768], replicated, may hold values from -0.21875 to 0.21875
- output_weight: float32 [768, 768], replicated, may hold values from -0.21875 to 0.21875
- feed_gain: float32 [768], replicated, may hold values from 0.5 to 1.5
- feed_weight: float32 [768, 4096], replicated, may hold values from -0.21875 to 0.21875
- down_weight: float32 [2048, 768], replicated, may hold values from -0.125 to 0.125
Outputs:
- layer_output: float32 [8, 1024, 768], P('rows', 'seq')
- input_grad: float32 [8, 1024, 768], P('rows', 'seq')
- mixer_gain_grad: float32 [768], replicated
- triple_weight_grad: float32 [768, 2304], P('rows', 'seq')
- rate_weight_grad: float32 [768, 12], replicated
- rate_bias_grad: float32 [12], replicated
- first_weight_grad: float32 [12, 64, 256], replicated
- first_bias_grad: float32 [12, 256], replicated
- second_weight_grad: float32 [12, 256, 64], replicated
- second_bias_grad: float32 [12, 64], replicated
- inner_gain_grad: float32 [12, 64], replicated
- inner_shift_grad: float32 [12, 64], replicated
- gate_weight_grad: float32 [768, 768], P('rows', 'seq')
- output_weight_grad: float32 [768, 768], P('rows', 'seq')
- feed_gain_grad: float32 [768], replicated
- feed_weight_grad: float32 [768, 4096], P('rows', 'seq')
- down_weight_grad: float32 [2048, 768], P('rows', 'seq')
Inputs may be any that keep to these rules, and one draw needn't show every extreme that they name: `doc_lengths`: each row holds 4 documents in order, each starting on a multiple of 16 tokens and taking ceil(length / 16) whole mini-batches; together they take exactly the row's 1024 / 16 mini-batches. The second document of every row starts in the row's first 256 tokens and ends in its last 256.
All inputs are finite; a program needn't handle non-finite values.
Results may differ from a plain program's by a relative error of at most 0.0003.
Values sent between devices are 32-bit elements; how exact they have to be, the bound alone decides.
No kernel may reach another device: no remote copies, remote signals or barrier semaphores. Data moves between devices by JAX's collectives and lax.ppermute only.
A program may use at most 256 MiB of HBM per device.

v0:
```python
import functools
import jax
import jax.numpy as jnp
from jax import lax
from jax.experimental import pallas as pl
from jax.experimental.pallas import tpu as pltpu
from jax.sharding import PartitionSpec as P

HEAD = 64
INNER = 256
MB = 16
EPS = 1e-06
RTP = 0.7978845608028654
F32 = jnp.float32
BF16 = jnp.bfloat16
LANES = 128
BASE_RATE = 0.1
FWD_COST = 1_500_000_000
BWD_COST = 2_000_000_000


def hi_lo(value):
    high = value.astype(BF16)
    return high, (value - high.astype(F32)).astype(BF16)


def hi_mid_lo(value):
    high = value.astype(BF16)
    rest = value - high.astype(F32)
    mid = rest.astype(BF16)
    return high, mid, (rest - mid.astype(F32)).astype(BF16)


def fold_all(value):
    total = value[:MB]
    for at in range(MB, value.shape[0], MB):
        total = total + value[at : at + MB]
    return total


def six_left(high, mid, low):
    return rows2(high, high, high, mid, mid, low)


def six_right(high, mid, low):
    return rows2(high, mid, low, high, mid, high)


def three_times(value):
    return jnp.concatenate([value, value[:, :HEAD]], axis=1)


def mm(left, right):
    return lax.dot_general(left, right, (((1,), (0,)), ((), ())), preferred_element_type=F32)


def mm_nt(left, right):
    return lax.dot_general(left, right, (((1,), (1,)), ((), ())), preferred_element_type=F32)


def mm_tn(left, right):
    return lax.dot_general(left, right, (((0,), (0,)), ((), ())), preferred_element_type=F32)


def rows2(*parts):
    return jnp.concatenate(parts, axis=0)


def fold(value):
    return value[:MB] + value[MB:]


def half_turn(value):
    return pltpu.roll(value, HEAD, 1)


def both_halves(value):
    return value + half_turn(value)


def lane_of(shape):
    return lax.broadcasted_iota(jnp.int32, shape, 1)


def pick(block, unit):
    tile = block[:, (unit // 2) * LANES : (unit // 2 + 1) * LANES]
    turned = half_turn(tile)
    low_half = lane_of(tile.shape) < HEAD
    if unit % 2 == 0:
        return jnp.where(low_half, tile, turned)
    return jnp.where(low_half, turned, tile)


def pack(parts):
    tiles = []
    for at in range(0, len(parts), 2):
        left = parts[at]
        right = parts[at + 1] if at + 1 < len(parts) else jnp.zeros_like(left)
        tiles.append(jnp.where(lane_of(left.shape) < HEAD, left, right))
    return jnp.concatenate(tiles, axis=1) if len(tiles) > 1 else tiles[0]


def mean_dup(value):
    return jnp.sum(value, axis=1, keepdims=True) * (1.0 / LANES)


def gelu_parts(z):
    z2 = z * z
    t = jnp.tanh(z * (RTP + (RTP * 0.044715) * z2))
    one_t = 0.5 + 0.5 * t
    sech = (1.0 - t) * one_t
    inner = RTP + (RTP * 0.134145) * z2
    act = z * one_t
    zs = z * sech
    slope = one_t + zs * inner
    return act, slope, t, zs, sech, inner


def gelu_curve(z, t, zs, sech, inner):
    return 2.0 * sech * inner + zs * ((2.0 * RTP * 0.134145) * z) - 2.0 * t * zs * inner * inner


def split3(high, low):
    return rows2(high, high, low)


def stack3(high, low):
    return rows2(high, low, high)


def lanes3(value):
    high, low = hi_lo(value)
    lane = lane_of(value.shape)
    return jnp.where((lane >= MB) & (lane < 2 * MB), low.astype(F32), high.astype(F32)).astype(BF16)


def interleave(works):
    works = list(works)
    while works:
        for work in list(works):
            try:
                next(work)
            except StopIteration:
                works.remove(work)


def rates_of(cols, bias_ref, heads, count):
    unit = 3 * heads
    tile = cols[:, (unit // 2) * LANES : (unit // 2 + 1) * LANES] + bias_ref[:1]
    sig = 0.5 + 0.5 * jnp.tanh(0.5 * tile)
    row = lax.broadcasted_iota(jnp.int32, tile.shape, 0)
    return jnp.where(row < count, (BASE_RATE / HEAD) * sig, 0.0), sig, HEAD * (unit % 2)


def put(refs, head, *values):
    for ref, value in zip(refs, values, strict=True):
        ref[head] = value


def take(refs, head):
    return [ref[head] for ref in refs]


def spread_lanes(column, width=LANES):
    return jnp.broadcast_to(column, (MB, width))


def fwd_ready(heads):
    shapes = [((5 * MB, 3 * HEAD), BF16), ((HEAD + 2 * MB, 3 * MB), BF16), ((MB, 3 * MB), F32)] + [((MB, LANES), F32)] * 4
    return [pltpu.VMEM((heads,) + shape, dtype) for shape, dtype in shapes]


def fwd_left(heads):
    shapes = [((2 * MB, INNER), BF16), ((2 * MB, LANES), BF16), ((MB, 3 * MB), F32), ((MB, LANES), F32), ((MB, LANES), F32)]
    return [pltpu.VMEM((heads,) + shape, dtype) for shape, dtype in shapes]


def fwd_kernel(heads, steps, resets_ref, counts_ref, qkv_ref, gate_ref, bias_ref, gain_ref, shift_ref, w1i, b1i, w2i, b2i,
               gated_ref, mixed_ref, s1_ref, s2_ref, z1_ref, zq_ref, m_ref, d2_ref, x_ref, y_ref, r_ref, rq_ref,
               w1, b1, w2, b2, *ready):
    block = pl.program_id(0)
    count = len(fwd_ready(heads))
    ready, left = (ready[:count], ready[count : 2 * count]), ready[2 * count :]
    left = (left[: len(left) // 2], left[len(left) // 2 :])
    lane = lane_of((MB, LANES))
    row = lax.broadcasted_iota(jnp.int32, (MB, LANES), 0)
    lane48 = lane_of((MB, 3 * MB))
    row48 = lax.broadcasted_iota(jnp.int32, (MB, 3 * MB), 0)
    causal = (lane >= HEAD) & (lane < HEAD + MB) & (row <= lane - HEAD)

    def rows_of(i):
        return pl.ds(pl.multiple_of(i * MB, MB), MB)

    def prepare(i, refs):
        qkv = qkv_ref[rows_of(i), :]
        rates, _, rate_lane = rates_of(qkv, bias_ref, heads, counts_ref[block * steps + i])

        def work(h):
            q = pick(qkv, h)
            k = pick(qkv, heads + h)
            v = pick(qkv, 2 * heads + h)
            e = spread_lanes(rates[:, rate_lane + h : rate_lane + h + 1])
            yield
            coef = gain_ref[h] * (shift_ref[h] - v + k)
            khi, klo = hi_lo(k)
            qhi, qlo = hi_lo(q)
            left_a = three_times(rows2(*hi_mid_lo(k), qhi, qlo))
            qsplit = jnp.where(lane < HEAD, qhi.astype(F32), qlo.astype(F32)).astype(BF16)
            zero = jnp.zeros((HEAD, LANES), BF16)
            kq = fold(mm_nt(rows2(khi, klo), rows2(zero, qsplit, zero[: HEAD - MB])))
            yield
            left_d = e * jnp.where(lane < HEAD, k, jnp.where(causal, kq + 1.0, jnp.where((lane >= HEAD + MB) & (lane < HEAD + 2 * MB), 1.0, 0.0)))
            left_d3 = jnp.transpose(stack3(*hi_lo(left_d)))[: HEAD + 2 * MB]
            erow = jnp.transpose(e)[:MB, :]
            e3 = jnp.where(lax.rem(lane48, MB) <= row48, jnp.concatenate([erow, erow, erow], axis=1), 0.0)
            yield
            put(refs, h, left_a, left_d3, e3, e, q, coef, spread_lanes(mean_dup(coef)))

        return [work(h) for h in range(heads)]

    def advance(i, refs, left):
        def work(h):
            left_a, left_d3, e3, e, q, coef, coef_mean = take(refs, h)
            gain = gain_ref[h]
            gain2 = gain * gain
            w1f = w1[h]
            w2f = w2[h]
            w1s = rows2(*hi_mid_lo(w1f))
            w2hi, w2mid, w2lo = hi_mid_lo(w2f)
            w2s = rows2(w2hi, w2mid)
            s1_ref[i, h] = w1s[: 2 * HEAD]
            s2_ref[i, h] = w2s
            b1v = b1[h]
            b2v = b2[h]
            z = mm(left_a, w1s)
            yield
            z1 = fold_all(z[: 3 * MB]) + b1v
            act, slope = gelu_parts(z1)[:2]
            ahi, alo, arest = hi_mid_lo(act)
            z2 = fold_all(mm_nt(rows2(ahi, alo, arest), rows2(w2s, w2lo, jnp.zeros((HEAD, INNER), BF16))))
            yield
            z2 = both_halves(z2[:, :LANES] + z2[:, LANES:]) + b2v
            yield
            g2z = gain2 * z2
            inv = lax.rsqrt(mean_dup(z2 * z2) + EPS)
            m1 = mean_dup(g2z)
            m2 = mean_dup(g2z * z2)
            m3 = mean_dup(coef * z2)
            yield
            x = z2 * inv
            g = gain2 * x + coef
            d2 = inv * (g - (inv * m1 + coef_mean) - x * (inv * inv * m2 + inv * m3))
            d2hi, d2lo = hi_lo(d2)
            m = fold(mm(rows2(d2hi, d2lo), w2s))
            yield
            d1 = m * slope
            u = mm(left_d3, split3(*hi_lo(d1)))
            yield
            w1[h] = w1f - u[:HEAD]
            b1[h] = b1v - u[HEAD + MB :]
            ed2 = e * d2
            w2[h] = w2f - mm(jnp.transpose(six_left(*hi_mid_lo(ed2)))[:HEAD], six_right(ahi, alo, arest))
            b2[h] = b2v - jnp.sum(ed2, axis=0, keepdims=True)
            z1_ref[i, h] = z1
            zq_ref[i, h] = fold(z[3 * MB :]) + b1v - u[HEAD : HEAD + MB]
            m_ref[i, h] = m
            d2_ref[i, h] = d2
            x_ref[i, h] = x
            r_ref[i, h] = spread_lanes(inv)
            put(left, h, rows2(ahi, alo), rows2(d2hi, d2lo), e3, q, b2v)

        return [work(h) for h in range(heads)]

    def finish(i, left, outs):
        def work(h):
            left_b, left_c, e3, q, b2v = take(left, h)
            ahi, alo = left_b[:MB], left_b[MB:]
            w2s = s2_ref[i, h]
            qact = gelu_parts(zq_ref[i, h])[0]
            qahi, qalo = hi_lo(qact)
            left_e = rows2(qahi, qalo)
            uq = fold(mm_nt(left_e, rows2(ahi, ahi, ahi))) + mm_nt(qahi, rows2(alo, alo, alo))
            z2q = fold(mm_nt(left_e, w2s))
            yield
            r3 = lanes3(e3 * (uq + 1.0))
            z2q = both_halves(z2q) + b2v - mm(r3, split3(left_c[:MB], left_c[MB:]))
            yield
            invq = lax.rsqrt(mean_dup(z2q * z2q) + EPS)
            yield
            y = z2q * invq
            outs[h] = q + gain_ref[h] * y + shift_ref[h]
            y_ref[i, h] = y
            rq_ref[i, h] = spread_lanes(invq)

        return [work(h) for h in range(heads)]

    def store(i, outs):
        mixed = pack(outs)
        mixed_ref[rows_of(i), :] = mixed
        gated_ref[rows_of(i), :] = gelu_parts(gate_ref[rows_of(i), :])[0] * mixed

    def step(i, now, later, parity):
        @pl.when(resets_ref[block * steps + i] == 1)
        def _():
            w1[...] = w1i[...]
            b1[...] = jnp.broadcast_to(b1i[...], b1.shape)
            w2[...] = w2i[...]
            b2[...] = jnp.broadcast_to(b2i[...], b2.shape)

        outs = [None] * heads
        behind = jnp.maximum(i - 1, 0)
        interleave(advance(i, now, left[parity]) + finish(behind, left[1 - parity], outs) + prepare(jnp.minimum(i + 1, steps - 1), later))
        store(behind, outs)

    interleave(prepare(0, ready[0]))

    def pair(at, carry):
        step(2 * at, ready[0], ready[1], 0)
        step(2 * at + 1, ready[1], ready[0], 1)
        return carry

    lax.fori_loop(0, steps // 2, pair, 0)
    outs = [None] * heads
    interleave(finish(steps - 1, left[1], outs))
    store(steps - 1, outs)


def bwd_ready(heads):
    halves = [(2 * MB, LANES), (HEAD + MB, 6 * MB), (2 * MB, INNER), (2 * MB, INNER), (2 * MB, INNER), (2 * MB, INNER), (2 * MB, LANES), (HEAD, 6 * MB)]
    wide = [(MB, INNER)] * 4
    rest = [(MB, LANES)] * 11
    shapes = [(shape, BF16) for shape in halves] + [(shape, F32) for shape in wide + rest]
    return [pltpu.VMEM((heads,) + shape, dtype) for shape, dtype in shapes]


def bwd_left(heads):
    shapes = [((LANES, INNER), BF16), ((4 * MB, INNER), BF16), ((2 * MB, INNER), BF16)] + [((MB, LANES), F32)] * 5
    return [pltpu.VMEM((heads,) + shape, dtype) for shape, dtype in shapes]


def bwd_kernel(heads, steps, first_block, begun, resets_ref, counts_ref, qkv_ref, bias_ref, cot_ref, gain_ref, shift_ref,
               s1_ref, s2_ref, z1_ref, zq_ref, m_ref, d2_ref, x_ref, y_ref, r_ref, rq_ref, *refs):
    before = refs[:10] if begun else None
    dqkv_ref, w1, b1, w2, b2, gw1, gb1, gw2, gb2, ggain, gshift, *ready = refs[10 if begun else 0 :]
    count = len(bwd_ready(heads))
    ready, left = (ready[:count], ready[count : 2 * count]), ready[2 * count :]
    left = (left[: len(left) // 2], left[len(left) // 2 :])
    blocks = pl.num_programs(0)
    block = first_block + blocks - 1 - pl.program_id(0)
    lane = lane_of((MB, LANES))
    lane48 = lane_of((MB, 3 * MB))
    row48 = lax.broadcasted_iota(jnp.int32, (MB, 3 * MB), 0)
    causal3 = row48 <= lax.rem(lane48, MB)
    counted = causal3 & (lane48 < MB)

    @pl.when(pl.program_id(0) == 0)
    def _():
        for at, ref in enumerate((w1, b1, w2, b2, gw1, gb1, gw2, gb2, ggain, gshift)):
            ref[...] = before[at][...] if begun else jnp.zeros_like(ref)

    def rows_of(i):
        return pl.ds(pl.multiple_of(i * MB, MB), MB)

    def rates_at(i, qkv):
        return rates_of(qkv, bias_ref, heads, counts_ref[block * steps + i])

    def prepare(i, refs):
        qkv = qkv_ref[rows_of(i), :]
        rates, sigs, rate_lane = rates_at(i, qkv)
        cots = cot_ref[rows_of(i), :]

        def work(h):
            gain = gain_ref[h]
            gain2 = gain * gain
            q = pick(qkv, h)
            k = pick(qkv, heads + h)
            v = pick(qkv, 2 * heads + h)
            cot = pick(cots, h)
            ecol = rates[:, rate_lane + h : rate_lane + h + 1]
            e = spread_lanes(ecol)
            e256 = spread_lanes(ecol, INNER)
            e3 = jnp.where(causal3, spread_lanes(ecol, 3 * MB), 0.0)
            khi, klo = hi_lo(k)
            qhi, qlo = hi_lo(q)
            left_k = rows2(khi, klo)
            qsplit = jnp.where(lane < HEAD, qhi.astype(F32), qlo.astype(F32)).astype(BF16)
            kq3 = fold(mm_nt(left_k, rows2(qsplit, qsplit, qsplit))) + 1.0
            yield
            pt3 = lanes3(e3 * kq3)
            ones = jnp.where(lane < HEAD + MB, 1.0, 0.0)
            qone = hi_lo(jnp.where(lane < HEAD, q, ones))
            kone = hi_lo(jnp.where(lane < HEAD, k, ones))
            left_q = jnp.transpose(rows2(stack3(*qone), stack3(*kone)))[: HEAD + MB]
            z1 = z1_ref[i, h]
            zq = zq_ref[i, h]
            m = m_ref[i, h]
            d2 = d2_ref[i, h]
            x = x_ref[i, h]
            y = y_ref[i, h]
            invq = rq_ref[i, h]
            act, slope, t, zs, sech, inner = gelu_parts(z1)
            curve = gelu_curve(z1, t, zs, sech, inner)
            qact, qslope = gelu_parts(zq)[:2]
            ahi, alo = hi_lo(act)
            qahi, qalo = hi_lo(qact)
            d1 = m * slope
            d1hi, d1lo = hi_lo(d1)
            d2hi, d2lo = hi_lo(d2)
            dy = gain * cot
            dy_mean = mean_dup(dy)
            dyy_mean = mean_dup(dy * y)
            yield
            dz2q = invq * (dy - dy_mean - y * dyy_mean)
            zhi, zlo = hi_lo(dz2q)
            dqa = fold(mm(rows2(zhi, zlo), s2_ref[i, h]))
            yield
            left_a = rows2(ahi, alo)
            aq3 = fold(mm_nt(left_a, rows2(qahi, qahi, qahi))) + mm_nt(ahi, rows2(qalo, qalo, qalo)) + 1.0
            yield
            zsplit = jnp.where(lane < HEAD, zhi.astype(F32), zlo.astype(F32)).astype(BF16)
            drt3 = -fold(mm_nt(rows2(d2hi, d2lo), rows2(zsplit, zsplit, zsplit)))
            yield
            rt3 = lanes3(e3 * aq3)
            dd2 = -mm(rt3, split3(zhi, zlo))
            de = jnp.sum(jnp.where(counted, drt3 * aq3, 0.0), axis=1, keepdims=True)
            du2t = e3 * drt3
            du2t_hi, du2t_lo = hi_lo(du2t[:, :MB])
            dqa = dqa + mm_tn(rows2(du2t_hi, du2t_lo, du2t_hi), split3(ahi, alo))
            yield
            da = mm(lanes3(du2t), split3(qahi, qalo))
            dzq = dqa * qslope
            zqhi, zqlo = hi_lo(dzq)
            dpt3 = -(fold(mm_nt(rows2(d1hi, d1lo), rows2(zqhi, zqhi, zqhi))) + mm_nt(d1hi, rows2(zqlo, zqlo, zqlo)))
            yield
            dd1 = -mm(pt3, split3(zqhi, zqlo))
            de = de + jnp.sum(jnp.where(counted, dpt3 * kq3, 0.0), axis=1, keepdims=True)
            du1t = e3 * dpt3
            du1t_hi, du1t_lo = hi_lo(du1t[:, :MB])
            dq = cot + mm_tn(rows2(du1t_hi, du1t_lo, du1t_hi), split3(khi, klo))
            dk = mm(lanes3(du1t), split3(qhi, qlo))
            yield
            left_2 = jnp.transpose(rows2(stack3(zhi, zlo), stack3(d2hi, d2lo)))[:HEAD]
            target = shift_ref[h] - v + k
            g = gain2 * x + gain * target
            put(
                refs, h, left_k, left_q, left_a, rows2(qahi, qalo), rows2(zqhi, zqlo), rows2(*hi_lo(e256 * d1)), rows2(*hi_lo(e * d2)), left_2,
                slope, m * curve, dd1, da,
                dd2, dq, dk, spread_lanes(de), dz2q, cot * y, cot, g, spread_lanes(mean_dup(g * x)), 2.0 * gain * x + target, e,
            )

        return [work(h) for h in range(heads)]

    def advance(i, refs, left):
        following = resets_ref[jnp.minimum(block * steps + i + 1, resets_ref.shape[0] - 1)]
        carry_on = jnp.where(following == 1, 0.0, 1.0)

        def work(h):
            left_k, left_q, left_a, left_qa, left_zq, left_ed1, left_ed2, left_2, slope, mcurve, dd1, da, *rest = take(refs, h)
            dd2, dq, dk, de, dz2q, gain_part, cot, g, mgx, gain_factor, e = rest
            gain = gain_ref[h]
            gain2 = gain * gain
            s2 = s2_ref[i, h]
            m = m_ref[i, h]
            d2 = d2_ref[i, h]
            x = x_ref[i, h]
            inv = r_ref[i, h]
            w1f = w1[h] * carry_on
            w2f = w2[h] * carry_on
            b1v = b1[h] * carry_on
            b2v = b2[h] * carry_on
            w1s = rows2(*hi_lo(w1f))
            w2s = rows2(*hi_lo(w2f))
            de1 = -(fold(mm(left_k, w1s)) + b1v)
            yield
            e256 = jnp.concatenate([e, e], axis=1)
            dd1 = dd1 + e256 * de1
            dm = dd1 * slope
            dmhi, dmlo = hi_lo(dm)
            de2 = -(both_halves(fold(mm_nt(left_a, w2s))) + b2v)
            back = both_halves(fold(mm_nt(rows2(dmhi, dmlo), s2)))
            yield
            dd2 = dd2 + e * de2 + back
            yield
            q1 = mean_dup(dd2)
            q2 = mean_dup(dd2 * x)
            dr_r = mean_dup(dd2 * d2)
            yield
            dg = inv * (dd2 - q1 - x * q2)
            dx = dg * gain2 - inv * (dd2 * mgx + g * q2)
            x1 = mean_dup(dx)
            x2 = mean_dup(dx * x)
            yield
            dz2 = inv * (dx - x1 - x * x2) - x * inv * dr_r
            dz2hi, dz2lo = hi_lo(dz2)
            da = da - fold(mm(left_ed2, w2s)) + fold(mm(rows2(dz2hi, dz2lo), s2))
            yield
            dz1 = dd1 * mcurve + da * slope
            z1hi, z1lo = hi_lo(dz1)
            zqhi, zqlo = left_zq[:MB], left_zq[MB:]
            grads = mm(left_q, rows2(split3(zqhi, zqlo), split3(z1hi, z1lo)))
            yield
            w1[h] = w1f + grads[:HEAD]
            b1[h] = b1v + grads[HEAD:]
            ahi, alo = left_a[:MB], left_a[MB:]
            qahi, qalo = left_qa[:MB], left_qa[MB:]
            left_3 = jnp.transpose(stack3(dz2hi, dz2lo))[:HEAD]
            w2[h] = w2f + mm(left_2, rows2(split3(qahi, qalo), split3(dmhi, dmlo))) + mm(left_3, split3(ahi, alo))
            b2[h] = b2v + jnp.sum(dz2q + dz2, axis=0, keepdims=True)
            dgg = dg * gain
            rate_terms = m * slope * de1
            rate_terms = rate_terms[:, :LANES] + rate_terms[:, LANES:] + 0.5 * (d2 * de2)
            ggain[h] += gain_part + dg * gain_factor
            gshift[h] += cot + dgg
            put(left, h, w1s, rows2(left_zq, z1hi, z1lo), left_ed1, dq, dk + dgg, -dgg, de, rate_terms)

        return [work(h) for h in range(heads)]

    def finish(i, left, dqs, dks, dvs, des):
        def work(h):
            w1s, left_z, left_ed1, dq, dk, dv, de, rate_terms = take(left, h)
            dkw = fold(mm_nt(left_ed1, w1s))
            to_rows = mm_nt(left_z, s1_ref[i, h])
            yield
            dqs[h] = dq + both_halves(fold(to_rows[: 2 * MB]))
            dks[h] = dk + both_halves(fold(to_rows[2 * MB :]) - dkw)
            dvs[h] = dv
            des[h] = de[:, :1] + jnp.sum(rate_terms, axis=1, keepdims=True)

        return [work(h) for h in range(heads)]

    def store(i, dqs, dks, dvs, des):
        rates, sigs, _ = rates_at(i, qkv_ref[rows_of(i), :])
        dpre = jnp.zeros((MB, LANES), F32)
        for h in range(heads):
            dpre = jnp.where(lax.rem(lane, HEAD) == h, des[h], dpre)
        dqkv_ref[rows_of(i), :] = pack(dqs + dks + dvs + [dpre * rates * (1.0 - sigs)])

    def step(i, now, later, parity):
        outs = [[None] * heads for _ in range(4)]
        behind = jnp.minimum(i + 1, steps - 1)
        interleave(advance(i, now, left[parity]) + finish(behind, left[1 - parity], *outs) + prepare(jnp.maximum(i - 1, 0), later))
        store(behind, *outs)

        @pl.when(resets_ref[block * steps + i] == 1)
        def _():
            gw1[...] += w1[...]
            gb1[...] += b1[...]
            gw2[...] += w2[...]
            gb2[...] += b2[...]

    interleave(prepare(steps - 1, ready[0]))

    def pair(at, carry):
        step(steps - 1 - 2 * at, ready[0], ready[1], 0)
        step(steps - 2 - 2 * at, ready[1], ready[0], 1)
        return carry

    lax.fori_loop(0, steps // 2, pair, 0)
    outs = [[None] * heads for _ in range(4)]
    interleave(finish(0, left[1], *outs))
    store(0, *outs)


def tiles_of(count):
    return -(-count // 2) * LANES


def state_scratch(heads):
    return [
        pltpu.VMEM((heads, HEAD, INNER), F32),
        pltpu.VMEM((heads, MB, INNER), F32),
        pltpu.VMEM((heads, HEAD, INNER), F32),
        pltpu.VMEM((heads, MB, LANES), F32),
    ]


def saved_shapes(total, heads):
    return [
        ((total, heads, LANES, INNER), BF16),
        ((total, heads, LANES, INNER), BF16),
        ((total, heads, MB, INNER), F32),
        ((total, heads, MB, INNER), F32),
        ((total, heads, MB, INNER), F32),
        ((total, heads, MB, LANES), F32),
        ((total, heads, MB, LANES), F32),
        ((total, heads, MB, LANES), F32),
        ((total, heads, MB, LANES), F32),
        ((total, heads, MB, LANES), F32),
    ]


def whole_spec(shape):
    zeros = (0,) * len(shape)
    return pl.BlockSpec(shape, lambda i, *_: zeros)


def own_weights_kernel(heads, owners, all_heads, me_ref, triple_ref, rate_ref, gate_ref, mixer_ref, own_gate_ref):
    for owner in range(owners):
        mine = [head for head in range(owner * heads, (owner + 1) * heads)]

        @pl.when(me_ref[0] == owner)
        def _(mine=mine):
            lane = lane_of((triple_ref.shape[0], LANES))
            none = jnp.zeros(lane.shape, F32)

            def units(ref, group):
                return [pick(ref, group * all_heads + head) if head < all_heads else none for head in mine]

            rate = none
            for at, head in enumerate(mine):
                if head < all_heads:
                    column = jnp.broadcast_to(rate_ref[:, head : head + 1], lane.shape)
                    rate = jnp.where(lax.rem(lane, HEAD) == at, column, rate)
            mixer_ref[...] = pack(units(triple_ref, 0) + units(triple_ref, 1) + units(triple_ref, 2) + [rate])
            own_gate_ref[...] = pack(units(gate_ref, 0))


def own_weights(me, owners, heads, triple, rate, gate, interpret=False):
    block = LANES
    width = triple.shape[0]
    row_spec = lambda columns: pl.BlockSpec((block, columns), lambda i, *_: (i, 0))
    wide = (tiles_of(3 * heads + 1), tiles_of(heads))
    return pl.pallas_call(
        functools.partial(own_weights_kernel, heads, owners, rate.shape[1]),
        grid_spec=pltpu.PrefetchScalarGridSpec(
            num_scalar_prefetch=1,
            grid=(width // block,),
            in_specs=[row_spec(triple.shape[1]), row_spec(rate.shape[1]), row_spec(gate.shape[1])],
            out_specs=[row_spec(columns) for columns in wide],
        ),
        out_shape=[jax.ShapeDtypeStruct((width, columns), F32) for columns in wide],
        compiler_params=pltpu.CompilerParams(dimension_semantics=("arbitrary",), vmem_limit_bytes=32 * 1024 * 1024),
    )(me, triple, rate, gate)


def chain_forward(resets, counts, cols, gate, bias, gain, shift, w1i, b1i, w2i, b2i, steps=8):
    heads = gain.shape[0]
    total = resets.shape[0]
    blocks = total // steps
    token_spec = lambda width: pl.BlockSpec((steps * MB, width), lambda i, *_: (i, 0))
    saved = saved_shapes(total, heads)
    saved_specs = [pl.BlockSpec((steps,) + s[1:], lambda i, *_: (i, 0, 0, 0)) for s, _ in saved]
    params = (bias, gain, shift, w1i, b1i, w2i, b2i)
    wide = tiles_of(heads)
    out = pl.pallas_call(
        functools.partial(fwd_kernel, heads, steps),
        grid_spec=pltpu.PrefetchScalarGridSpec(
            num_scalar_prefetch=2,
            grid=(blocks,),
            in_specs=[token_spec(cols.shape[1]), token_spec(wide)] + [whole_spec(p.shape) for p in params],
            out_specs=[token_spec(wide), token_spec(wide)] + saved_specs,
            scratch_shapes=state_scratch(heads) + 2 * fwd_ready(heads) + 2 * fwd_left(heads),
        ),
        out_shape=[jax.ShapeDtypeStruct((total * MB, wide), F32)] * 2 + [jax.ShapeDtypeStruct(s, d) for s, d in saved],
        compiler_params=pltpu.CompilerParams(dimension_semantics=("arbitrary",), vmem_limit_bytes=56 * 1024 * 1024),
        cost_estimate=pl.CostEstimate(flops=FWD_COST * total, bytes_accessed=1 << 20, transcendentals=0),
    )(resets, counts, cols, gate, *params)
    return out[0], out[1], out[2:]


def chain_backward(resets, counts, cols, bias, cot, gain, shift, saved, part=(0, 8), before=None, steps=8):
    heads = gain.shape[0]
    total = resets.shape[0]
    first = total // steps * part[0] // 8
    blocks = total // steps * part[1] // 8 - first
    last = first + blocks - 1
    token_spec = lambda width: pl.BlockSpec((steps * MB, width), lambda i, *_: (last - i, 0))
    wide = tiles_of(3 * heads + 1)
    saved_specs = [pl.BlockSpec((steps,) + s.shape[1:], lambda i, *_: (last - i, 0, 0, 0)) for s in saved]
    state_shapes = [(heads, HEAD, INNER), (heads, MB, INNER), (heads, HEAD, INNER), (heads, MB, LANES)]
    kept = state_shapes + state_shapes + [(heads, MB, LANES), (heads, MB, LANES)]
    kept_specs = [whole_spec(s) for s in kept]
    before = [] if before is None else list(before)
    out = pl.pallas_call(
        functools.partial(bwd_kernel, heads, steps, first, bool(before)),
        grid_spec=pltpu.PrefetchScalarGridSpec(
            num_scalar_prefetch=2,
            grid=(blocks,),
            in_specs=[token_spec(cols.shape[1]), whole_spec(bias.shape), token_spec(cot.shape[1]), whole_spec(gain.shape), whole_spec(shift.shape)]
            + saved_specs
            + kept_specs[: len(before)],
            out_specs=[pl.BlockSpec((steps * MB, wide), lambda i, *_: (blocks - 1 - i, 0))] + kept_specs,
            scratch_shapes=2 * bwd_ready(heads) + 2 * bwd_left(heads),
        ),
        out_shape=[jax.ShapeDtypeStruct((blocks * steps * MB, wide), F32)] + [jax.ShapeDtypeStruct(s, F32) for s in kept],
        compiler_params=pltpu.CompilerParams(dimension_semantics=("arbitrary",), vmem_limit_bytes=56 * 1024 * 1024),
        cost_estimate=pl.CostEstimate(flops=BWD_COST * blocks * steps, bytes_accessed=1 << 20, transcendentals=0),
    )(resets, counts, cols, bias, cot, gain, shift, *saved, *before)
    return out[0], out[1:]


HEADS = 12
high = lax.Precision.HIGH


def dot(left, right):
    return jnp.dot(left, right, precision=high)


def dot_t(left, right):
    return lax.dot_general(left, right, (((1,), (1,)), ((), ())), precision=high)


def t_dot(left, right):
    return lax.dot_general(left, right, (((0,), (0,)), ((), ())), precision=high)


def swap(value, axis, mask):
    count = lax.axis_size(axis)
    return lax.ppermute(value, axis, [(source, source ^ mask) for source in range(count)])


def bits_of(axis):
    count = lax.axis_size(axis)
    return [1 << at for at in reversed(range(count.bit_length() - 1))]


def upper_of(axis, mask):
    return (lax.axis_index(axis) & mask) != 0


def gather(value, axis, beside=None):
    shape = value.shape
    for done, mask in enumerate(bits_of(axis)):
        other = swap(value, axis, mask)
        if beside is not None and done == 0:
            other, beside = lax.optimization_barrier((other, beside))
        upper = upper_of(axis, mask)
        value = jnp.stack([jnp.where(upper, other, value), jnp.where(upper, value, other)], axis=done)
    value = value.reshape((-1,) + shape)
    return value if beside is None else (value, beside)


def gather_by_distance(value, axis):
    shape = value.shape
    for done, mask in enumerate(bits_of(axis)):
        value = jnp.stack([value, swap(value, axis, mask)], axis=done)
    return value.reshape((-1,) + shape)


def halves(value, axis, mask, dim):
    upper = upper_of(axis, mask)
    lower_half = lax.index_in_dim(value, 0, dim, keepdims=False)
    upper_half = lax.index_in_dim(value, 1, dim, keepdims=False)
    return jnp.where(upper, upper_half, lower_half), jnp.where(upper, lower_half, upper_half)


def row_stages(first=()):
    masks = bits_of("rows")
    order = [mask for mask in first if mask in masks] + [mask for mask in reversed(masks) if mask not in first]
    stages = []
    left = list(masks)
    for mask in order:
        stages.append(("rows", mask, left.index(mask)))
        left.remove(mask)
    return stages


def run_stages(value, stages):
    for axis, mask, dim in stages:
        keep, sent = halves(value, axis, mask, dim)
        value = keep + swap(sent, axis, mask)
    return value


def row_blocks(value):
    count = lax.axis_size("rows")
    return value.reshape((2,) * len(bits_of("rows")) + (value.shape[0] // count,) + value.shape[1:])


def low_bit_blocks(value, other=False):
    n = lax.axis_size("seq")
    share = value.shape[1] // n
    bit = (lax.axis_index("seq") & 1) ^ int(other)
    return jnp.stack([lax.dynamic_slice_in_dim(value, (2 * at + bit) * share, share, 1) for at in range(n // 2)])


def even_first(value):
    n = lax.axis_size("seq")
    share = value.shape[1] // n
    blocks = [value[:, at * share : (at + 1) * share] for at in list(range(0, n, 2)) + list(range(1, n, 2))]
    return jnp.concatenate(blocks, axis=1)


def own_half(value, other=False):
    share = value.shape[1] // 2
    bit = (lax.axis_index("seq") & 1) ^ int(other)
    return lax.dynamic_slice_in_dim(value, bit * share, share, 1)


def columns_to_tokens(value, width):
    n = lax.axis_size("seq")
    tokens = value.shape[0] // n
    moved = lax.all_to_all(value.reshape(n, tokens, -1), "seq", 0, 0)
    return moved.transpose(1, 0, 2).reshape(tokens, -1)[:, :width]


def tokens_to_columns(value):
    n = lax.axis_size("seq")
    tokens = value.shape[0]
    moved = lax.all_to_all(value.reshape(tokens, n, -1).transpose(1, 0, 2), "seq", 0, 0)
    return moved.reshape(n * tokens, -1)


def block_marks(lengths, total):
    block_counts = (lengths + MB - 1) // MB
    begins = (jnp.cumsum(block_counts, dtype=jnp.int32) - block_counts)[None, :]
    index = jnp.arange(total, dtype=jnp.int32)[:, None]
    resets = jnp.any(index == begins, axis=1).astype(jnp.int32)
    inside = jnp.clip(lengths[None, :] - MB * (index - begins), 0, MB)
    return resets, jnp.sum(jnp.where(index >= begins, inside, 0), axis=1)


def own_heads(value, axis, per_head, groups=1):
    n = lax.axis_size("seq")
    me = lax.axis_index("seq")
    count = -(-HEADS // n)
    shape = value.shape
    if n * count == HEADS:
        share = count * per_head
        parts = [lax.dynamic_slice_in_dim(value, g * HEADS * per_head + me * share, share, axis) for g in range(groups)]
        return jnp.concatenate(parts, axis=axis) if groups > 1 else parts[0]
    value = value.reshape(shape[:axis] + (groups, HEADS * per_head) + shape[axis + 1 :])
    pads = [(0, 0)] * value.ndim
    pads[axis + 1] = (0, (n * count - HEADS) * per_head)
    value = jnp.pad(value, pads)
    value = lax.dynamic_slice_in_dim(value, me * count * per_head, count * per_head, axis + 1)
    return value.reshape(shape[:axis] + (groups * count * per_head,) + shape[axis + 1 :])


def pad_columns(value, width):
    return jnp.pad(value, ((0, 0), (0, width - value.shape[1])))


def together(*values):
    return lax.optimization_barrier(values)


def local(
    layer_input,
    doc_lengths,
    output_grad,
    mixer_gain,
    triple_weight,
    rate_weight,
    rate_bias,
    first_weight,
    first_bias,
    second_weight,
    second_bias,
    inner_gain,
    inner_shift,
    gate_weight,
    output_weight,
    feed_gain,
    feed_weight,
    down_weight,
):
    n = lax.axis_size("seq")
    n_rows = lax.axis_size("rows")
    me = lax.axis_index("seq")
    heads = -(-HEADS // n)
    _, tokens, width = layer_input.shape
    span = tokens * n
    ff = down_weight.shape[0]
    head_cols = heads * HEAD
    x = layer_input[0]
    cot = output_grad[0]
    resets, counts = block_marks(doc_lengths[0], span // MB)

    inv = lax.rsqrt(jnp.mean(x * x, axis=-1, keepdims=True) + EPS)
    xhat = x * inv
    normed = xhat * mixer_gain
    split = tiles_of(3 * heads + 1)
    own_mixer, own_gate = own_weights(me[None], n, heads, triple_weight, rate_weight, gate_weight)
    rate_lane = HEAD * (3 * heads % 2)
    bias = jnp.pad(own_heads(rate_bias, 0, 1), (rate_lane, LANES - heads - rate_lane))[None, :]

    def per_head(value, times):
        value = own_heads(value, 0, 1)
        return jnp.concatenate([value] * times, axis=1)[:, None, :]

    gain = per_head(inner_gain, 2)
    shift = per_head(inner_shift, 2)
    w1i = own_heads(first_weight, 0, 1)
    b1i = per_head(first_bias, 1)
    w2t = own_heads(second_weight, 0, 1).transpose(0, 2, 1)
    w2i = w2t - jnp.mean(w2t, axis=1, keepdims=True)
    b2i = per_head(second_bias - jnp.mean(second_bias, axis=1, keepdims=True), 2)
    normed_row, beside = gather(normed, "seq", (own_mixer, own_gate, bias, gain, shift, w1i, b1i, w2i, b2i, resets, counts))
    own_mixer, own_gate, bias, gain, shift, w1i, b1i, w2i, b2i, resets, counts = beside
    normed_row = normed_row.reshape(span, width)
    cols = jnp.dot(normed_row, own_mixer, precision=lax.Precision.HIGHEST)
    gate_pre = dot(normed_row, own_gate)
    gated_cols, mixed, saved = chain_forward(resets, counts, cols, gate_pre, bias, gain, shift, w1i, b1i, w2i, b2i)

    gated = columns_to_tokens(gated_cols[:, :head_cols], width)
    dhidden = dot_t(cot, down_weight)
    gated, dhidden = together(gated, dhidden)
    middle = x + dot(gated, output_weight)
    inv2 = lax.rsqrt(jnp.mean(middle * middle, axis=-1, keepdims=True) + EPS)
    mhat = middle * inv2
    second = mhat * feed_gain
    both = dot(second, feed_weight)
    left, right = both[:, :ff], both[:, ff:]
    sig = jax.nn.sigmoid(left)
    silu = left * sig
    hidden = silu * right
    narrow_stages = row_stages()
    cot_split = even_first(cot)
    down_sum = row_blocks(t_dot(hidden, own_half(cot_split)) + swap(t_dot(hidden, own_half(cot_split, True)), "seq", 1))
    down_keep, down_sent = halves(down_sum, *narrow_stages[0])
    down_other = swap(down_sent, *narrow_stages[0][:2])

    dboth = jnp.concatenate([dhidden * right * (sig + silu * (1.0 - sig)), dhidden * silu], axis=1)
    dsecond = dot_t(dboth, feed_weight)
    feed_gain_part = jnp.sum(dsecond * mhat, axis=0)
    dmhat = dsecond * feed_gain
    dmiddle = cot + inv2 * (dmhat - mhat * jnp.mean(dmhat * mhat, axis=-1, keepdims=True))
    dgated = tokens_to_columns(pad_columns(dot_t(dmiddle, output_weight), n * head_cols))

    second_row = gather_by_distance(second, "seq").reshape(span, width)
    feed_moved = jnp.stack([low_bit_blocks(dboth), swap(low_bit_blocks(dboth, True), "seq", 1)], axis=1)
    dmiddle_split = even_first(dmiddle)
    output_sum = row_blocks(t_dot(gated, own_half(dmiddle_split)) + swap(t_dot(gated, own_half(dmiddle_split, True)), "seq", 1))
    output_keep, output_sent = halves(output_sum, *narrow_stages[0])
    feed_masks = bits_of("seq")[:-1]
    feed_moved = feed_moved.reshape((2,) * len(feed_masks) + (2, tokens, -1))
    for mask in feed_masks[:0:-1]:
        keep, sent = halves(feed_moved, "seq", mask, feed_masks.index(mask))
        feed_moved = jnp.stack([keep, swap(sent, "seq", mask)], axis=feed_masks.index(mask))
        feed_moved = feed_moved.reshape(feed_moved.shape[: feed_masks.index(mask)] + (-1, tokens, feed_moved.shape[-1]))
    feed_keep, feed_sent = halves(feed_moved, "seq", feed_masks[0], 0)
    dgated, output_sent, feed_sent = together(dgated, output_sent, feed_sent)
    feed_other = swap(feed_sent, "seq", feed_masks[0])
    output_other = swap(output_sent, *narrow_stages[0][:2])

    dgated = dgated[:, :head_cols]
    gate_act, gate_slope = gelu_parts(gate_pre[:, :head_cols])[:2]
    dmixed = pad_columns(dgated * gate_act, tiles_of(heads))
    dgate = dgated * mixed[:, :head_cols] * gate_slope
    backward = functools.partial(chain_backward, resets, counts, cols, bias, dmixed, gain, shift, saved)
    part_a, kept = backward(part=(5, 8))

    part_a, kept, down_other, output_other, feed_other, dgate = together(part_a, kept, down_other, output_other, feed_other, dgate)
    dboth_row = jnp.stack([feed_keep, feed_other]).reshape(span, -1)
    feed_cols = dboth_row.shape[1]
    gate_part = t_dot(normed_row, dgate)
    feed = row_blocks(jnp.concatenate([t_dot(second_row, dboth_row), gate_part], axis=1))
    dnormed_gate = dot_t(dgate, own_gate[:, :head_cols])
    feed_stages = row_stages()
    feed_keep, feed_sent = halves(feed, *feed_stages[0])
    narrow = jnp.concatenate([down_keep + down_other, output_keep + output_other], axis=-2)
    narrow_keep, narrow_sent = halves(narrow, *narrow_stages[1])
    kept, feed_sent, narrow_sent, dnormed_gate = together(kept, feed_sent, narrow_sent, dnormed_gate)
    feed_other = swap(feed_sent, *feed_stages[0][:2])
    narrow_other = swap(narrow_sent, *narrow_stages[1][:2])
    part_b, kept = backward(part=(2, 5), before=kept)
    part_b, hidden, middle = together(part_b, hidden, middle)
    layer_output = middle + dot(hidden, down_weight)

    part_b, kept, narrow_other, feed_other = together(part_b, kept, narrow_other, feed_other)
    feed_keep, feed_sent = halves(feed_keep + feed_other, *feed_stages[1])
    narrow_keep, narrow_sent = halves(narrow_keep + narrow_other, *narrow_stages[2])
    kept, feed_sent, narrow_sent = together(kept, feed_sent, narrow_sent)
    feed_other = swap(feed_sent, *feed_stages[1][:2])
    narrow_other = swap(narrow_sent, *narrow_stages[2][:2])
    part_c, kept = backward(part=(0, 2), before=kept)

    part_c, kept, narrow_other, feed_other = together(part_c, kept, narrow_other, feed_other)
    feed = run_stages(feed_keep + feed_other, feed_stages[2:])
    narrow = run_stages(narrow_keep + narrow_other, narrow_stages[3:])
    seq_masks = bits_of("seq")[:-1]
    narrow = jnp.stack(jnp.split(narrow, n // 2, axis=1)).reshape((2,) * len(seq_masks) + (narrow.shape[0], -1))
    narrow = run_stages(narrow, [("seq", mask, seq_masks.index(mask)) for mask in reversed(seq_masks)])
    down_weight_grad, output_weight_grad = narrow[: ff // n_rows], narrow[ff // n_rows :]
    feed_weight_grad, gate_weight_grad = feed[:, :feed_cols], feed[:, feed_cols:]

    dcols = jnp.concatenate([part_c, part_b, part_a])
    triple_part = t_dot(normed_row, dcols)
    triple_blocks = row_blocks(triple_part)
    triple_sum = run_stages(triple_blocks, row_stages())
    dcols, triple_part = together(dcols, triple_part)
    dnormed = dot_t(dcols, own_mixer) + dnormed_gate
    dnormed = dnormed.reshape((2,) * len(bits_of("seq")) + (tokens, width))
    seq_order = [("seq", mask, bits_of("seq").index(mask)) for mask in reversed(bits_of("seq"))]
    dnormed = run_stages(dnormed, seq_order[:-1])
    dnormed_keep, dnormed_sent = halves(dnormed, *seq_order[-1])

    rate_tile = dcols[:, 3 * head_cols - rate_lane :][:, :LANES]
    rate_part = t_dot(rate_tile, normed_row)[rate_lane : rate_lane + heads]
    mixer_gain_part = jnp.sum(triple_part * own_mixer, axis=1)
    mixer_gain_part = (mixer_gain_part + jnp.sum(gate_part * own_gate[:, :head_cols], axis=1)) / mixer_gain
    gw1, gb1, gw2, gb2, ggain, gshift = kept[4:]
    lane_sums = jnp.sum(rate_tile, axis=0)[rate_lane : rate_lane + heads]
    narrow_rows = jnp.concatenate(
        [gb2[:, 0, :HEAD], jnp.sum(ggain, axis=1)[:, :HEAD], jnp.sum(gshift, axis=1)[:, :HEAD], lane_sums[:, None]], axis=1
    )
    pieces = [
        gw1.reshape(-1, INNER),
        gw2.reshape(-1, INNER),
        gb1[:, 0],
        pad_columns(narrow_rows, INNER),
        rate_part.reshape(-1, INNER),
        jnp.stack([mixer_gain_part, feed_gain_part]).reshape(-1, INNER),
    ]
    lengths = [piece.shape[0] for piece in pieces]
    rest = jnp.concatenate(pieces[2:])
    rest = jnp.pad(rest, ((0, -sum(lengths) % (n_rows * 8)), (0, 0)))
    small = jnp.concatenate(pieces[:2] + [rest])
    small, dnormed_sent = together(small, dnormed_sent)
    dnormed_other = swap(dnormed_sent, *seq_order[-1][:2])
    small = run_stages(row_blocks(small), row_stages())
    small = gather(small, "rows")
    small, dnormed_other = together(small, dnormed_other)
    small = gather(small, "seq").reshape(n, -1, INNER)
    starts = [sum(lengths[:at]) for at in range(len(lengths))]
    small = [small[:, start : start + length] for start, length in zip(starts, lengths)]
    first_weight_grad = small[0].reshape(n * heads, HEAD, INNER)[:HEADS]
    second_weight_grad = small[1].reshape(n * heads, HEAD, INNER)[:HEADS].transpose(0, 2, 1)
    first_bias_grad = small[2].reshape(n * heads, INNER)[:HEADS]
    narrow_rows = small[3].reshape(n * heads, INNER)[:HEADS]
    second_bias_grad, inner_gain_grad, inner_shift_grad = (narrow_rows[:, HEAD * at : HEAD * (at + 1)] for at in range(3))
    rate_bias_grad = narrow_rows[:, 3 * HEAD]
    rate_weight_grad = small[4].reshape(n * heads, width)[:HEADS].T
    gains = jnp.sum(small[5], axis=0).reshape(2, width)

    dxhat = (dnormed_keep + dnormed_other) * mixer_gain
    input_grad = dmiddle + inv * (dxhat - xhat * jnp.mean(dxhat * xhat, axis=-1, keepdims=True))

    triple_every = gather(triple_sum, "seq")
    share = 3 * width // n
    if n * heads == HEADS and share % head_cols == 0:
        blocks = []
        for at in range(share // head_cols):
            block = me * (share // head_cols) + at
            columns = lax.dynamic_slice(triple_every, (block % n, 0, block // n * head_cols), (1, triple_every.shape[1], head_cols))
            blocks.append(columns[0])
        triple_weight_grad = jnp.concatenate(blocks, axis=1)
    else:
        every = triple_every[:, :, : 3 * head_cols].reshape(n, -1, 3, head_cols).transpose(1, 2, 0, 3)
        every = every.reshape(every.shape[0], 3, -1)[:, :, :width].reshape(every.shape[0], 3 * width)
        triple_weight_grad = lax.dynamic_slice_in_dim(every, me * share, share, 1)
    if n * heads != HEADS:
        every = gather(gate_weight_grad, "seq").transpose(1, 0, 2)
        every = every.reshape(every.shape[0], -1)[:, :width]
        gate_weight_grad = lax.dynamic_slice_in_dim(every, me * (width // n), width // n, 1)

    return (
        layer_output[None],
        input_grad[None],
        gains[0],
        triple_weight_grad,
        rate_weight_grad,
        rate_bias_grad,
        first_weight_grad,
        first_bias_grad,
        second_weight_grad,
        second_bias_grad,
        inner_gain_grad,
        inner_shift_grad,
        gate_weight_grad,
        output_weight_grad,
        gains[1],
        feed_weight_grad,
        down_weight_grad,
    )


def solution(mesh):
    tokens = P("rows", "seq", None)
    shard = P("rows", "seq")
    in_specs = (tokens, P("rows", None), tokens) + (P(),) * 15
    out_specs = (tokens, tokens, P(), shard) + (P(),) * 8 + (shard, shard, P(), shard, shard)
    return jax.shard_map(local, mesh=mesh, in_specs=in_specs, out_specs=out_specs, check_vma=False)
```

profile of v0, /device:TPU:0, one launch (start us, length us, event | category | flops | bytes accessed | tf_op | source)
XLA Modules:
  0.0 486.2 jit_solution(14154831446571160229)
XLA Ops:
  2.1 2.1 fusion.26
  4.3 3.0 collective-permute-start
  12.6 3.0 copy-done.7
  15.6 1.7 copy-done.8
  19.8 1.7 bitcast_subtract_fusion
  21.5 3.6 collective-permute-done
  28.6 2.4 fusion.57
  34.7 2.4 fusion.62.gate_ref
  37.7 9.2 %fusion.61.qkv_ref = f32[1024,640]{1,0:T(8,128)} fusion(f32[1024,768]{1,0:T(8,128)S(1)} %bitcast.277, f32[768,640]{1,0:T(8,128)S(1)} %copy-done.3), kind=kOutput, calls=%fused_computation.217 | convolution fusion | flops 6039797760 | bytes 7733248 | tf_op jit(solution)/shard_map/dot_general | solution.py:893
  46.9 67.8 %shard_map.306 = (f32[1024,256]{1,0:T(8,128)}, f32[1024,256]{1,0:T(8,128)}, bf16[64,3,128,256]{3,2,1,0:T(8,128)(2,1)}, bf16[64,3,128,256]{3,2,1,0:T(8,128)(2,1)}...) custom-call(s32[64]{0:T(128)} %convert_element_type.11.resets_ref, ...), custom_call_target="tpu_custom_call" | custom-call | flops 96000000000 | bytes 1048576 | tf_op jit(solution)/shard_map/pallas_call | solution.py:645
  114.7 2.4 copy.162
  117.1 3.5 all-to-all-start
  120.7 2.3 pad_maximum_fusion.14
  123.0 6.8 %fusion.48 = f32[256,2048]{1,0:T(8,128)} fusion(f32[2048,768]{1,0:T(8,128)} %param.35, f32[1,256,768]{2,1,0:T(8,128)S(1)} %copy-done.41), kind=kOutput, calls=%fused_computation.205 | convolution fusion | flops 2415919104 | bytes 9175040 | tf_op jit(solution)/shard_map/dot_general | solution.py:701
  129.8 2.5 all-to-all-done
  133.1 2.7 multiply_reduce_fusion.5
  137.0 9.5 %fusion.63 = f32[256,4096]{1,0:T(8,128)S(1)} fusion(f32[256,768]{1,0:T(8,128)} %multiply_multiply_fusion.1, f32[768,4096]{1,0:T(8,128)} %param.34), kind=kOutput, calls=%fused_computation.219 | convolution fusion | flops 4831838208 | bytes 17563648 | tf_op jit(solution)/shard_map/dot_general | solution.py:697
  146.4 4.1 add_multiply_fusion
  150.6 3.5 fusion.30
  154.2 8.8 %multiply_reduce_fusion.2 = (f32[768]{0:T(1024)S(1)}, f32[256]{0:T(256)S(1)}, f32[256,768]{1,0:T(8,128)}) fusion(f32[256,768]{1,0:T(8,128)S(1)} %get-tuple-element.215, f32[256]{0:T(256)S(1)} %add_rsqrt_fusion, f32[768]{0:T(1024)S(1)} %copy-done.68, f32[768,4096]{1,0:T(8,128)S(1)} %bitcast.282, f32[256,2048]{1,0:T(8,128)} %get-tuple-element.369, ...), kind=kOutput, calls=%fused_computation.88 | convolution fusion | flops 4834065408 | bytes 18358272 | tf_op jit(solution)/shard_map/dot_general | solution.py:701
  162.9 2.4 fusion.15
  169.1 1.8 fusion.33
  171.8 2.2 fusion.64
  174.0 3.5 all-to-all-start.1
  178.2 3.1 maximum_bitcast_fusion
  182.3 17.3 %all-to-all-done.1 = f32[4,256,192]{1,2,0:T(8,128)S(1)} async-done(((f32[4,256,192]{1,2,0:T(8,128)}), f32[4,256,192]{1,2,0:T(8,128)S(1)}, u32[]{:S(2)}, u32[]{:S(2)}) %all-to-all-start.1) | async-done | bytes 786464 | tf_op jit(solution)/shard_map/all_to_all | solution.py:801
  199.9 3.1 fusion.50
  203.1 2.2 convolution_add_fusion.2
  206.2 4.8 broadcast_select_fusion
  213.0 1.7 collective-permute-start.6
  214.8 3.9 convolution_add_fusion
  220.6 39.9 %shard_map.307 = (f32[384,640]{1,0:T(8,128)}, f32[3,64,256]{2,1,0:T(8,128)}, f32[3,16,256]{2,1,0:T(8,128)}, f32[3,64,256]{2,1,0:T(8,128)}, f32[3,16,128]{2,1,0:T...) custom-call(s32[64]{0:T(128)} %convert_element_type.11.resets_ref, ...), custom_call_target="tpu_custom_call" | custom-call | flops 48000000000 | bytes 1048576 | tf_op jit(solution)/shard_map/pallas_call | solution.py:674
  263.5 3.1 fusion.24
  266.7 2.7 multiply_reduce_fusion.3
  269.5 1.9 bitcast_add_fusion.2
  272.0 7.6 %fusion.7 = f32[768,1024]{1,0:T(8,128)S(1)} fusion(f32[1,2,256,1024]{3,2,1,0:T(8,128)} %bitcast.33, f32[1,2,256,1024]{3,2,1,0:T(8,128)S(1)} %copy-done.60, f32[2,1,256,768]{3,2,0,1:T(8,128)} %bitcast.32, f32[2,1,256,768]{3,2,0,1:T(8,128)S(1)} %copy-done.61), kind=kOutput, calls=%fused_computation.36 | convolution fusion | flops 4833673216 | bytes 10485760 | tf_op jit(solution)/shard_map/dot_general | solution.py:705
  280.2 1.7 select_bitcast_fusion.1
  283.1 1.7 collective-permute-start.11
  286.4 40.6 %shard_map.308 = (f32[384,640]{1,0:T(8,128)}, f32[3,64,256]{2,1,0:T(8,128)}, f32[3,16,256]{2,1,0:T(8,128)}, f32[3,64,256]{2,1,0:T(8,128)}, f32[3,16,128]{2,1,0:T...) custom-call(s32[64]{0:T(128)} %convert_element_type.11.resets_ref, ...), custom_call_target="tpu_custom_call" | custom-call | flops 48000000000 | bytes 1048576 | tf_op jit(solution)/shard_map/pallas_call | solution.py:674
  327.0 6.8 %fusion.12 = f32[1,256,768]{2,1,0:T(8,128)} fusion(f32[256,768]{1,0:T(8,128)S(1)} %copy-done.15, f32[256,2048]{1,0:T(8,128)S(1)} %copy-done.13, f32[2048,768]{1,0:T(8,128)} %param.35), kind=kOutput, calls=%fused_computation.51 | convolution fusion | flops 2416115712 | bytes 9961472 | tf_op jit(solution)/shard_map/dot_general | solution.py:697
  335.7 2.3 bitcast_add_fusion
  338.8 2.6 collective-permute-start.12
  341.4 28.5 %shard_map.309 = (f32[256,640]{1,0:T(8,128)}, f32[3,64,256]{2,1,0:T(8,128)}, f32[3,16,256]{2,1,0:T(8,128)}, f32[3,64,256]{2,1,0:T(8,128)}, f32[3,16,128]{2,1,0:T...) custom-call(s32[64]{0:T(128)} %convert_element_type.11.resets_ref, ...), custom_call_target="tpu_custom_call" | custom-call | flops 32000000000 | bytes 1048576 | tf_op jit(solution)/shard_map/pallas_call | solution.py:674
  370.2 2.1 collective-permute-done.13
  374.3 1.7 collective-permute-start.30
  379.8 4.5 fusion.65
  389.1 4.0 convolution_add_fusion.1
  398.4 1.9 multiply_reduce_fusion
  400.9 2.2 fusion.28
  404.1 1.7 pad_maximum_fusion.16
  408.6 1.7 copy.192
  410.4 1.7 bitcast_add_fusion.5
  412.5 1.7 bitcast_add_fusion.1
  415.8 2.1 collective-permute-start.25
  417.9 5.4 %collective-permute-done.15 = f32[2,2,56,256]{3,2,1,0:T(8,128)S(1)} collective-permute-done((f32[2,2,56,256]{3,2,1,0:T(8,128)S(1)}, f32[2,2,56,256]{3,2,1,0:T(8,128)S(1)}, u32[]{:S(2)}, u32[]{:S(2)}) %collective-permute-start.15) | collective-permute-done | bytes 229408 | tf_op jit(solution)/shard_map/ppermute | solution.py:710
  423.4 2.0 collective-permute-start.16
  428.0 4.0 collective-permute-done.16
  432.0 2.3 collective-permute-start.17
  434.5 2.9 collective-permute-done.17
  437.4 2.1 collective-permute-start.18
  440.9 8.2 %collective-permute-done.18 = f32[56,256]{1,0:T(8,128)S(1)} collective-permute-done((f32[56,256]{1,0:T(8,128)S(1)}, f32[56,256]{1,0:T(8,128)S(1)}, u32[]{:S(2)}, u32[]{:S(2)}) %collective-permute-start.18) | collective-permute-done | bytes 57376 | tf_op jit(solution)/shard_map/ppermute | solution.py:710
  449.2 4.2 collective-permute-done.26
  456.9 6.1 %collective-permute-done.27 = f32[96,640]{1,0:T(8,128)S(1)} collective-permute-done((f32[96,640]{1,0:T(8,128)S(1)}, f32[96,640]{1,0:T(8,128)S(1)}, u32[]{:S(2)}, u32[]{:S(2)}) %collective-permute-start.27) | collective-permute-done | bytes 245792 | tf_op jit(solution)/shard_map/ppermute | solution.py:710
  464.5 11.8 %collective-permute-done.22 = f32[8,56,256]{2,1,0:T(8,128)S(1)} collective-permute-done((f32[8,56,256]{2,1,0:T(8,128)S(1)}, f32[8,56,256]{2,1,0:T(8,128)S(1)}, u32[]{:S(2)}, u32[]{:S(2)}) %collective-permute-start.22) | collective-permute-done | bytes 458784 | tf_op jit(solution)/shard_map/ppermute | solution.py:710
  (347 shorter events, 81.0 us)
Async XLA Ops:
  0.7 132.5 %copy-start = (f32[768,768]{1,0:T(8,128)S(1)}, f32[768,768]{1,0:T(8,128)}, u32[]{:S(2)}) copy-start(f32[768,768]{1,0:T(8,128)} %param.32) | copy-start | bytes 7077892
  0.7 6.6 %copy-start.76 = (f32[12,64]{1,0:T(8,128)S(1)}, f32[12,64]{1,0:T(8,128)}, u32[]{:S(2)}) copy-start(f32[12,64]{1,0:T(8,128)} %param.28) | copy-start | bytes 9220
  0.7 10.8 %copy-start.82 = (f32[12]{0:T(128)S(1)}, f32[12]{0:T(128)}, u32[]{:S(2)}) copy-start(f32[12]{0:T(128)} %param.24) | copy-start | bytes 148
  0.7 10.9 %copy-start.71 = (f32[768,12]{0,1:T(8,128)S(1)}, f32[768,12]{0,1:T(8,128)}, u32[]{:S(2)}) copy-start(f32[768,12]{0,1:T(8,128)} %param.23) | copy-start | bytes 110596
  0.7 11.1 %copy-start.83 = (s32[1,4]{1,0:T(1,128)S(1)}, s32[1,4]{1,0:T(1,128)}, u32[]{:S(2)}) copy-start(s32[1,4]{1,0:T(1,128)} %param.19) | copy-start | bytes 52
  2.1 23.0 %copy-start.72 = (f32[256]{0:T(256)}, f32[256]{0:T(256)S(1)}, u32[]{:S(2)}) copy-start(f32[256]{0:T(256)S(1)} %add_rsqrt_fusion.1) | copy-start | bytes 3076
  4.3 20.8 %collective-permute-start = (f32[256,768]{1,0:T(8,128)}, f32[256,768]{1,0:T(8,128)}, u32[]{:S(2)}, u32[]{:S(2)}) collective-permute-start(f32[256,768]{1,0:T(8,128)} %fusion.26), channel_id=1, source_target_pairs={{0,2},{1,3},{2,0},{3,1},{4,6},{5,7},{6,4},{7,5},{8,10},{9,11},{10,... | collective-permute-start | bytes 2359304 | tf_op jit(solution)/shard_map/ppermute | solution.py:710
  17.3 7.9 %copy-start.18 = (f32[1,256,768]{2,1,0:T(8,128)S(1)}, f32[1,256,768]{2,1,0:T(8,128)}, u32[]{:S(2)}) copy-start(f32[1,256,768]{2,1,0:T(8,128)} %param.18) | copy-start | bytes 2359300
  17.3 7.9 %copy-start.69 = (f32[768]{0:T(1024)S(1)}, f32[768]{0:T(1024)}, u32[]{:S(2)}) copy-start(f32[768]{0:T(1024)} %param.21) | copy-start | bytes 9220
  18.4 10.2 %copy-start.2 = (f32[768,640]{1,0:T(8,128)}, f32[768,640]{1,0:T(8,128)S(1)}, u32[]{:S(2)}) copy-start(f32[768,640]{1,0:T(8,128)S(1)} %get-tuple-element.153) | copy-start | bytes 5898244
  18.4 16.3 %copy-start.5 = (f32[768,256]{1,0:T(8,128)}, f32[768,256]{1,0:T(8,128)S(1)}, u32[]{:S(2)}) copy-start(f32[768,256]{1,0:T(8,128)S(1)} %get-tuple-element.155) | copy-start | bytes 2359300
  28.6 3.8 collective-permute-start.1
  117.1 15.1 %all-to-all-start = ((f32[4,256,192]{1,2,0:T(8,128)}), f32[4,256,192]{1,2,0:T(8,128)S(1)}, u32[]{:S(2)}, u32[]{:S(2)}) async-start(f32[4,256,192]{1,2,0:T(8,128)} %copy.162), calls=%async_computation | async-start | bytes 1572864 | tf_op jit(solution)/shard_map/all_to_all | solution.py:794
  135.8 45.5 %copy-start.14 = (f32[256,768]{1,0:T(8,128)}, f32[256,768]{1,0:T(8,128)S(1)}, u32[]{:S(2)}) copy-start(f32[256,768]{1,0:T(8,128)S(1)} %get-tuple-element.215) | copy-start | bytes 2359300
  137.0 17.1 %slice-start = ((s8[12582912]{0:T(1024)(128)(4,1)}), s8[4194304]{0:T(1024)(128)(4,1)S(1)}, s32[]{:S(2)}) async-start(s8[12582912]{0:T(1024)(128)(4,1)} %bitcast.281), calls=%async_computation.2 | async-start | bytes 8388608
  137.0 17.2 %slice-start.1 = ((s8[12582912]{0:T(1024)(128)(4,1)}), s8[4194304]{0:T(1024)(128)(4,1)S(1)}, s32[]{:S(2)}) async-start(s8[12582912]{0:T(1024)(128)(4,1)} %bitcast.281), calls=%async_computation.3 | async-start | bytes 8388608
  146.4 7.7 %slice-start.2 = ((s8[12582912]{0:T(1024)(128)(4,1)}), s8[4194304]{0:T(1024)(128)(4,1)S(1)}, s32[]{:S(2)}) async-start(s8[12582912]{0:T(1024)(128)(4,1)} %bitcast.281), calls=%async_computation.4 | async-start | bytes 8388608
  154.1 60.7 %collective-permute-start.4 = (f32[2048,384]{1,0:T(8,128)}, f32[2048,384]{1,0:T(8,128)}, u32[]{:S(2)}, u32[]{:S(2)}) collective-permute-start(f32[2048,384]{1,0:T(8,128)} %fusion.30), channel_id=1, source_target_pairs={{0,1},{1,0},{2,3},{3,2},{4,5},{5,4},{6,7},{7,6},{8,9},{9,8},{10,11... | collective-permute-start | bytes 9437192 | tf_op jit(solution)/shard_map/ppermute | solution.py:710
  154.1 8.8 %copy-start.20 = (f32[256,2048]{1,0:T(8,128)S(1)}, f32[256,2048]{1,0:T(8,128)}, u32[]{:S(2)}) copy-start(f32[256,2048]{1,0:T(8,128)} %get-tuple-element.369) | copy-start | bytes 6291460
  166.8 39.4 %collective-permute-start.3 = (f32[2,256,1024]{2,1,0:T(8,128)}, f32[2,256,1024]{2,1,0:T(8,128)}, u32[]{:S(2)}, u32[]{:S(2)}) collective-permute-start(f32[2,256,1024]{2,1,0:T(8,128)} %pad_maximum_fusion.6), channel_id=1, source_target_pairs={{0,1},{1,0},{2,3},{3,2},{4,5},{5,4},{6,7},{7,6},{8,9},{9,8},{10,11... | collective-permute-start | bytes 6291464 | tf_op jit(solution)/shard_map/ppermute | solution.py:710
  171.0 32.1 %collective-permute-start.2 = (f32[768,384]{1,0:T(8,128)}, f32[768,384]{1,0:T(8,128)}, u32[]{:S(2)}, u32[]{:S(2)}) collective-permute-start(f32[768,384]{1,0:T(8,128)} %fusion.33), channel_id=1, source_target_pairs={{0,1},{1,0},{2,3},{3,2},{4,5},{5,4},{6,7},{7,6},{8,9},{9,8},{10,11... | collective-permute-start | bytes 3538952 | tf_op jit(solution)/shard_map/ppermute | solution.py:710
  171.5 28.4 %collective-permute-start.8 = (f32[256,768]{1,0:T(8,128)}, f32[256,768]{1,0:T(8,128)}, u32[]{:S(2)}, u32[]{:S(2)}) collective-permute-start(f32[256,768]{1,0:T(8,128)} %multiply_multiply_fusion.1), channel_id=1, source_target_pairs={{0,2},{1,3},{2,0},{3,1},{4,6},{5,7},{6,4},{7,5},{8,10},{9,11},{10,... | collective-permute-start | bytes 2359304 | tf_op jit(solution)/shard_map/ppermute | solution.py:710
  174.0 25.5 %all-to-all-start.1 = ((f32[4,256,192]{1,2,0:T(8,128)}), f32[4,256,192]{1,2,0:T(8,128)S(1)}, u32[]{:S(2)}, u32[]{:S(2)}) async-start(f32[4,256,192]{1,2,0:T(8,128)} %bitcast.301), calls=%async_computation.1 | async-start | bytes 1572864 | tf_op jit(solution)/shard_map/all_to_all | solution.py:801
  182.3 17.6 %copy-start.59 = (f32[1,256,768]{2,1,0:T(8,128)S(1)}, f32[1,256,768]{2,1,0:T(8,128)}, u32[]{:S(2)}) copy-start(f32[1,256,768]{2,1,0:T(8,128)} %fusion.92) | copy-start | bytes 2359300
  203.1 68.3 %collective-permute-start.9 = (f32[2,256,768]{2,1,0:T(8,128)}, f32[2,256,768]{2,1,0:T(8,128)}, u32[]{:S(2)}, u32[]{:S(2)}) collective-permute-start(f32[2,256,768]{2,1,0:T(8,128)} %get-tuple-element.394), channel_id=1, source_target_pairs={{0,1},{1,0},{2,3},{3,2},{4,5},{5,4},{6,7},{7,6},{8,9},{9,8},{10,11... | collective-permute-start | bytes 4718600 | tf_op jit(solution)/shard_map/ppermute | solution.py:710
  206.2 4.8 copy-start.62
  212.7 48.2 %collective-permute-start.7 = (f32[2,256,1024]{2,1,0:T(8,128)}, f32[2,256,1024]{2,1,0:T(8,128)}, u32[]{:S(2)}, u32[]{:S(2)}) collective-permute-start(f32[2,256,1024]{2,1,0:T(8,128)} %get-tuple-element.188), channel_id=1, source_target_pairs={{0,2},{1,3},{2,0},{3,1},{4,6},{5,7},{6,4},{7,5},{8,10},{9,11},{10,... | collective-permute-start | bytes 6291464 | tf_op jit(solution)/shard_map/ppermute | solution.py:710
  213.0 47.5 %collective-permute-start.6 = (f32[2,2,96,384]{3,2,1,0:T(8,128)}, f32[2,2,96,384]{3,2,1,0:T(8,128)}, u32[]{:S(2)}, u32[]{:S(2)}) collective-permute-start(f32[2,2,96,384]{3,2,1,0:T(8,128)} %select_bitcast_fusion.14), channel_id=1, source_target_pairs={{0,4},{4,0},{8,12},{12,8},{16,20},{20,16},{24,28},{28,24},{1,5},{5... | collective-permute-start | bytes 1769480 | tf_op jit(solution)/shard_map/ppermute | solution.py:710
  220.1 42.3 %collective-permute-start.5 = (f32[2,2,256,384]{3,2,0,1:T(8,128)S(1)}, f32[2,2,256,384]{3,2,0,1:T(8,128)}, u32[]{:S(2)}, u32[]{:S(2)}) collective-permute-start(f32[2,2,256,384]{3,2,0,1:T(8,128)S(1)} %select_bitcast_fusion.3), channel_id=1, source_target_pairs={{0,4},{4,0},{8,12},{12,8},{16,20},{20,16},{24,28},{28,24},{1,5},{5... | collective-permute-start | bytes 4718600 | tf_op jit(solution)/shard_map/ppermute | solution.py:710
  263.5 18.3 %copy-start.50 = (f32[2,2,96,384]{3,2,1,0:T(8,128)}, f32[2,2,96,384]{3,2,1,0:T(8,128)S(1)}, u32[]{:S(2)}) copy-start(f32[2,2,96,384]{3,2,1,0:T(8,128)S(1)} %bitcast_add_fusion.7) | copy-start | bytes 1769476
  271.4 10.5 %copy-start.29 = (f32[2,2,256,384]{3,2,0,1:T(8,128)}, f32[2,2,256,384]{3,2,0,1:T(8,128)S(1)}, u32[]{:S(2)}) copy-start(f32[2,2,256,384]{3,2,0,1:T(8,128)S(1)} %bitcast_add_fusion.2) | copy-start | bytes 4718596
  283.1 43.9 %copy-start.15 = (f32[256,768]{1,0:T(8,128)S(1)}, f32[256,768]{1,0:T(8,128)}, u32[]{:S(2)}) copy-start(f32[256,768]{1,0:T(8,128)} %copy-done.14) | copy-start | bytes 2359300
  283.1 50.7 %collective-permute-start.11 = (f32[2,2,96,1216]{3,2,0,1:T(8,128)}, f32[2,2,96,1216]{3,2,0,1:T(8,128)}, u32[]{:S(2)}, u32[]{:S(2)}) collective-permute-start(f32[2,2,96,1216]{3,2,0,1:T(8,128)} %select_bitcast_fusion.1), channel_id=1, source_target_pairs={{0,4},{4,0},{8,12},{12,8},{16,20},{20,16},{24,28},{28,24},{1,5},{5... | collective-permute-start | bytes 5603336 | tf_op jit(solution)/shard_map/ppermute | solution.py:710
  284.9 49.0 %collective-permute-start.10 = (f32[2,352,384]{2,1,0:T(8,128)}, f32[2,352,384]{2,1,0:T(8,128)}, u32[]{:S(2)}, u32[]{:S(2)}) collective-permute-start(f32[2,352,384]{2,1,0:T(8,128)} %select_bitcast_fusion.6), channel_id=1, source_target_pairs={{0,8},{4,12},{8,0},{12,4},{16,24},{20,28},{24,16},{28,20},{1,9},{5... | collective-permute-start | bytes 3244040 | tf_op jit(solution)/shard_map/ppermute | solution.py:710
  327.0 6.8 %copy-start.30 = (f32[2,2,256,384]{3,2,0,1:T(8,128)S(1)}, f32[2,2,256,384]{3,2,0,1:T(8,128)}, u32[]{:S(2)}) copy-start(f32[2,2,256,384]{3,2,0,1:T(8,128)} %copy-done.29) | copy-start | bytes 4718596
  327.0 6.8 %copy-start.51 = (f32[2,2,96,384]{3,2,1,0:T(8,128)S(1)}, f32[2,2,96,384]{3,2,1,0:T(8,128)}, u32[]{:S(2)}) copy-start(f32[2,2,96,384]{3,2,1,0:T(8,128)} %copy-done.50) | copy-start | bytes 1769476
  338.2 34.1 %copy-start.36 = (f32[2,352,384]{2,1,0:T(8,128)S(1)}, f32[2,352,384]{2,1,0:T(8,128)}, u32[]{:S(2)}) copy-start(f32[2,352,384]{2,1,0:T(8,128)} %copy-done.35) | copy-start | bytes 3244036
  338.3 34.1 %collective-permute-start.13 = (f32[2,96,1216]{2,1,0:T(8,128)S(1)}, f32[2,96,1216]{2,1,0:T(8,128)}, u32[]{:S(2)}, u32[]{:S(2)}) collective-permute-start(f32[2,96,1216]{2,1,0:T(8,128)S(1)} %select_bitcast_fusion.8), channel_id=1, source_target_pairs={{0,8},{4,12},{8,0},{12,4},{16,24},{20,28},{24,16},{28,20},{1,9},{5... | collective-permute-start | bytes 2801672 | tf_op jit(solution)/shard_map/ppermute | solution.py:710
  338.8 31.4 %collective-permute-start.12 = (f32[352,384]{1,0:T(8,128)S(1)}, f32[352,384]{1,0:T(8,128)}, u32[]{:S(2)}, u32[]{:S(2)}) collective-permute-start(f32[352,384]{1,0:T(8,128)S(1)} %select_bitcast_fusion.15), channel_id=1, source_target_pairs={{0,16},{4,20},{8,24},{12,28},{16,0},{20,4},{24,8},{28,12},{1,17},{... | collective-permute-start | bytes 1622024 | tf_op jit(solution)/shard_map/ppermute | solution.py:710
  374.3 5.3 %copy-start.65 = (f32[256,640]{1,0:T(8,128)S(1)}, f32[256,640]{1,0:T(8,128)}, u32[]{:S(2)}) copy-start(f32[256,640]{1,0:T(8,128)} %get-tuple-element.261) | copy-start | bytes 1966084
  374.3 31.6 %collective-permute-start.30 = (f32[352,192]{1,0:T(8,128)S(1)}, f32[352,192]{1,0:T(8,128)}, u32[]{:S(2)}, u32[]{:S(2)}) collective-permute-start(f32[352,192]{1,0:T(8,128)S(1)} %slice_select_fusion), channel_id=1, source_target_pairs={{0,2},{1,3},{2,0},{3,1},{4,6},{5,7},{6,4},{7,5},{8,10},{9,11},{10,... | collective-permute-start | bytes 811016 | tf_op jit(solution)/shard_map/ppermute | solution.py:710
  378.2 47.3 %collective-permute-start.29 = (f32[96,1216]{1,0:T(8,128)}, f32[96,1216]{1,0:T(8,128)}, u32[]{:S(2)}, u32[]{:S(2)}) collective-permute-start(f32[96,1216]{1,0:T(8,128)} %select_bitcast_fusion.16), channel_id=1, source_target_pairs={{0,16},{4,20},{8,24},{12,28},{16,0},{20,4},{24,8},{28,12},{1,17},{... | collective-permute-start | bytes 1400840 | tf_op jit(solution)/shard_map/ppermute | solution.py:710
  379.7 7.7 %copy-start.21 = (f32[1024,640]{1,0:T(8,128)}, f32[1024,640]{1,0:T(8,128)S(1)}, u32[]{:S(2)}) copy-start(f32[1024,640]{1,0:T(8,128)S(1)} %constant_dynamic-update-slice_fusion) | copy-start | bytes 7864324
  386.7 23.6 %collective-permute-start.24 = (f32[2,2,96,640]{3,2,0,1:T(8,128)}, f32[2,2,96,640]{3,2,0,1:T(8,128)}, u32[]{:S(2)}, u32[]{:S(2)}) collective-permute-start(f32[2,2,96,640]{3,2,0,1:T(8,128)} %select_bitcast_fusion.7), channel_id=1, source_target_pairs={{0,4},{4,0},{8,12},{12,8},{16,20},{20,16},{24,28},{28,24},{1,5},{5... | collective-permute-start | bytes 2949128 | tf_op jit(solution)/shard_map/ppermute | solution.py:710
  395.2 5.2 %copy-start.70 = (f32[768]{0:T(1024)S(1)}, f32[768]{0:T(1024)}, u32[]{:S(2)}) copy-start(f32[768]{0:T(1024)} %param.21) | copy-start | bytes 9220
  395.2 5.3 %copy-start.77 = (f32[1,768]{1,0:T(1,128)S(1)}, f32[1,768]{1,0:T(1,128)}, u32[]{:S(2)}) copy-start(f32[1,768]{1,0:T(1,128)} %stack.166) | copy-start | bytes 9220
  395.2 16.9 %collective-permute-start.14 = (f32[2,256,768]{2,1,0:T(8,128)}, f32[2,256,768]{2,1,0:T(8,128)}, u32[]{:S(2)}, u32[]{:S(2)}) collective-permute-start(f32[2,256,768]{2,1,0:T(8,128)} %select_bitcast_fusion.2), channel_id=1, source_target_pairs={{0,1},{1,0},{2,3},{3,2},{4,5},{5,4},{6,7},{7,6},{8,9},{9,8},{10,11... | collective-permute-start | bytes 4718600 | tf_op jit(solution)/shard_map/ppermute | solution.py:710
  403.1 7.3 %copy-start.38 = (f32[2,2,1,96,640]{4,3,2,1,0:T(8,128)S(1)}, f32[2,2,1,96,640]{4,3,2,1,0:T(8,128)}, u32[]{:S(2)}) copy-start(f32[2,2,1,96,640]{4,3,2,1,0:T(8,128)} %copy-done.37) | copy-start | bytes 2949124
  403.1 7.3 %copy-start.40 = (f32[2,2,1,96,640]{4,3,2,1,0:T(8,128)S(1)}, f32[2,2,1,96,640]{4,3,2,1,0:T(8,128)}, u32[]{:S(2)}) copy-start(f32[2,2,1,96,640]{4,3,2,1,0:T(8,128)} %copy-done.39) | copy-start | bytes 2949124
  415.3 8.1 %collective-permute-start.15 = (f32[2,2,56,256]{3,2,1,0:T(8,128)S(1)}, f32[2,2,56,256]{3,2,1,0:T(8,128)S(1)}, u32[]{:S(2)}, u32[]{:S(2)}) collective-permute-start(f32[2,2,56,256]{3,2,1,0:T(8,128)S(1)} %select_bitcast_fusion.27), channel_id=1, source_target_pairs={{0,4},{4,0},{8,12},{12,8},{16,20},{20,16},{24,28},{28,24},{1,5},{5... | collective-permute-start | bytes 688136 | tf_op jit(solution)/shard_map/ppermute | solution.py:710
  415.8 18.6 %collective-permute-start.25 = (f32[2,96,640]{2,1,0:T(8,128)S(1)}, f32[2,96,640]{2,1,0:T(8,128)S(1)}, u32[]{:S(2)}, u32[]{:S(2)}) collective-permute-start(f32[2,96,640]{2,1,0:T(8,128)S(1)} %select_bitcast_fusion.19), channel_id=1, source_target_pairs={{0,8},{4,12},{8,0},{12,4},{16,24},{20,28},{24,16},{28,20},{1,9},{5... | collective-permute-start | bytes 1474568 | tf_op jit(solution)/shard_map/ppermute | solution.py:710
  423.4 8.6 %collective-permute-start.16 = (f32[2,56,256]{2,1,0:T(8,128)S(1)}, f32[2,56,256]{2,1,0:T(8,128)S(1)}, u32[]{:S(2)}, u32[]{:S(2)}) collective-permute-start(f32[2,56,256]{2,1,0:T(8,128)S(1)} %select_bitcast_fusion.30), channel_id=1, source_target_pairs={{0,8},{4,12},{8,0},{12,4},{16,24},{20,28},{24,16},{28,20},{1,9},{5... | collective-permute-start | bytes 344072 | tf_op jit(solution)/shard_map/ppermute | solution.py:710
  432.0 5.4 %collective-permute-start.17 = (f32[56,256]{1,0:T(8,128)S(1)}, f32[56,256]{1,0:T(8,128)S(1)}, u32[]{:S(2)}, u32[]{:S(2)}) collective-permute-start(f32[56,256]{1,0:T(8,128)S(1)} %select_bitcast_fusion.33), channel_id=1, source_target_pairs={{0,16},{4,20},{8,24},{12,28},{16,0},{20,4},{24,8},{28,12},{1,17},{... | collective-permute-start | bytes 172040 | tf_op jit(solution)/shard_map/ppermute | solution.py:710
  437.4 11.7 %collective-permute-start.18 = (f32[56,256]{1,0:T(8,128)S(1)}, f32[56,256]{1,0:T(8,128)S(1)}, u32[]{:S(2)}, u32[]{:S(2)}) collective-permute-start(f32[56,256]{1,0:T(8,128)S(1)} %bitcast_add_fusion.12), channel_id=1, source_target_pairs={{0,16},{4,20},{8,24},{12,28},{16,0},{20,4},{24,8},{28,12},{1,17},{... | collective-permute-start | bytes 172040 | tf_op jit(solution)/shard_map/ppermute | solution.py:710
  439.6 13.8 %collective-permute-start.26 = (f32[96,640]{1,0:T(8,128)S(1)}, f32[96,640]{1,0:T(8,128)S(1)}, u32[]{:S(2)}, u32[]{:S(2)}) collective-permute-start(f32[96,640]{1,0:T(8,128)S(1)} %select_bitcast_fusion.24), channel_id=1, source_target_pairs={{0,16},{4,20},{8,24},{12,28},{16,0},{20,4},{24,8},{28,12},{1,17},{... | collective-permute-start | bytes 737288 | tf_op jit(solution)/shard_map/ppermute | solution.py:710
  440.5 22.8 %collective-permute-start.21 = (f32[256,768]{1,0:T(8,128)S(1)}, f32[256,768]{1,0:T(8,128)S(1)}, u32[]{:S(2)}, u32[]{:S(2)}) collective-permute-start(f32[256,768]{1,0:T(8,128)S(1)} %select_bitcast_fusion.11), channel_id=1, source_target_pairs={{0,2},{1,3},{2,0},{3,1},{4,6},{5,7},{6,4},{7,5},{8,10},{9,11},{10,... | collective-permute-start | bytes 2359304 | tf_op jit(solution)/shard_map/ppermute | solution.py:710
  449.1 6.2 %collective-permute-start.19 = (f32[2,56,256]{2,1,0:T(8,128)S(1)}, f32[2,56,256]{2,1,0:T(8,128)S(1)}, u32[]{:S(2)}, u32[]{:S(2)}) collective-permute-start(f32[2,56,256]{2,1,0:T(8,128)S(1)} %pad_maximum_fusion.20), channel_id=1, source_target_pairs={{0,8},{4,12},{8,0},{12,4},{16,24},{20,28},{24,16},{28,20},{1,9},{5... | collective-permute-start | bytes 344072 | tf_op jit(solution)/shard_map/ppermute | solution.py:710
  453.4 9.6 %collective-permute-start.27 = (f32[96,640]{1,0:T(8,128)S(1)}, f32[96,640]{1,0:T(8,128)S(1)}, u32[]{:S(2)}, u32[]{:S(2)}) collective-permute-start(f32[96,640]{1,0:T(8,128)S(1)} %bitcast_add_fusion.11), channel_id=1, source_target_pairs={{0,2},{1,3},{2,0},{3,1},{4,6},{5,7},{6,4},{7,5},{8,10},{9,11},{10,... | collective-permute-start | bytes 737288 | tf_op jit(solution)/shard_map/ppermute | solution.py:710
  455.4 7.8 %collective-permute-start.20 = (f32[2,2,56,256]{3,2,0,1:T(8,128)S(1)}, f32[2,2,56,256]{3,2,0,1:T(8,128)S(1)}, u32[]{:S(2)}, u32[]{:S(2)}) collective-permute-start(f32[2,2,56,256]{3,2,0,1:T(8,128)S(1)} %pad_maximum_fusion.19), channel_id=1, source_target_pairs={{0,4},{4,0},{8,12},{12,8},{16,20},{20,16},{24,28},{28,24},{1,5},{5... | collective-permute-start | bytes 688136 | tf_op jit(solution)/shard_map/ppermute | solution.py:710
  463.1 14.5 %collective-permute-start.28 = (f32[2,96,640]{2,1,0:T(8,128)S(1)}, f32[2,96,640]{2,1,0:T(8,128)S(1)}, u32[]{:S(2)}, u32[]{:S(2)}) collective-permute-start(f32[2,96,640]{2,1,0:T(8,128)S(1)} %pad_maximum_fusion.15), channel_id=1, source_target_pairs={{0,1},{1,0},{2,3},{3,2},{4,5},{5,4},{6,7},{7,6},{8,9},{9,8},{10,11... | collective-permute-start | bytes 1474568 | tf_op jit(solution)/shard_map/ppermute | solution.py:710
  463.4 13.0 %collective-permute-start.22 = (f32[8,56,256]{2,1,0:T(8,128)S(1)}, f32[8,56,256]{2,1,0:T(8,128)S(1)}, u32[]{:S(2)}, u32[]{:S(2)}) collective-permute-start(f32[8,56,256]{2,1,0:T(8,128)S(1)} %bitcast.302), channel_id=1, source_target_pairs={{0,2},{1,3},{2,0},{3,1},{4,6},{5,7},{6,4},{7,5},{8,10},{9,11},{10,... | collective-permute-start | bytes 1376264 | tf_op jit(solution)/shard_map/ppermute | solution.py:710
  464.5 12.0 %copy-start.26 = (f32[256,768]{1,0:T(8,128)S(1)}, f32[256,768]{1,0:T(8,128)}, u32[]{:S(2)}) copy-start(f32[256,768]{1,0:T(8,128)} %copy-done.25) | copy-start | bytes 2359300
  476.5 2.5 collective-permute-start.23
  479.3 6.6 %copy-start.1 = (f32[768,768]{1,0:T(8,128)S(1)}, f32[768,768]{1,0:T(8,128)}, u32[]{:S(2)}) copy-start(f32[768,768]{1,0:T(8,128)} %param.32) | copy-start | bytes 7077892
  (56 other events, 140.5 us)
where the time goes:
time: 496 us; the launch traced here: 486 us
  Pallas kernels  178 us (36%)
  matrix products  83.8 us (17%)
  waiting for transfers between devices  73.3 us (15%)
  other arithmetic  68.7 us (14%)
  local copies, waits for them, and re-layouts  43.3 us (9%)
  starting transfers between devices  36.8 us (7%)
    pallas_call x3, Pallas kernels, chain_backward(): pl.pallas_call(functools.partial(bwd_kernel, heads, steps, first, bool(be...  109 us
    pallas_call x1, Pallas kernels, chain_forward(): pl.pallas_call(functools.partial(fwd_kernel, heads, steps), grid_spec=plt...  67.8 us
    ppermute x31, waiting for transfers between devices, swap(): lax.ppermute(value, axis, [(source, source ^ mask) for source in range(co...  53.5 us
    ppermute x31, starting transfers between devices, swap(): lax.ppermute(value, axis, [(source, source ^ mask) for source in range(co...  29.8 us
    dot_general x8, matrix products, t_dot(): lax.dot_general(left, right, (((0,), (0,)), ((), ())), precision=high)  28.5 us
    dot_general x5, matrix products, dot_t(): lax.dot_general(left, right, (((1,), (1,)), ((), ())), precision=high)  24.9 us
    dot_general x4, matrix products, dot(): return jnp.dot(left, right, precision=high)  21.3 us
    unnamed x180, local copies, waits for them, and re-layouts  20.1 us
  transfers between devices with their start and end apart: 33, of which 17 were waited for; matrix products, arithmetic and copies ran while one was open for 23% of the time, Pallas kernels for 23%

commit v1 on v0

--- a/solution.py
+++ b/solution.py
@@ -615,7 +615,7 @@
             own_gate_ref[...] = pack(units(gate_ref, 0))
 
 
-def own_weights(me, owners, heads, triple, rate, gate, interpret=False):
+def own_weights(me, owners, heads, triple, rate, gate):
     block = LANES
     width = triple.shape[0]
     row_spec = lambda columns: pl.BlockSpec((block, columns), lambda i, *_: (i, 0))
@@ -633,7 +633,7 @@
     )(me, triple, rate, gate)
 
 
-def chain_forward(resets, counts, cols, gate, bias, gain, shift, w1i, b1i, w2i, b2i, steps=8):
+def chain_forward(resets, counts, cols, gate, bias, gain, shift, w1i, b1i, w2i, b2i, steps=16):
     heads = gain.shape[0]
     total = resets.shape[0]
     blocks = total // steps

time: 496 us -> 494 us (level)
  no operation moved by 1% of the time
where the time goes in v1:
time: 494 us; the launch traced here: 485 us
  Pallas kernels  177 us (36%)
  matrix products  83.8 us (17%)
  waiting for transfers between devices  73.3 us (15%)
  other arithmetic  68.7 us (14%)
  local copies, waits for them, and re-layouts  43.3 us (9%)
  starting transfers between devices  36.7 us (7%)
    pallas_call x3, Pallas kernels, chain_backward(): pl.pallas_call(functools.partial(bwd_kernel, heads, steps, first, bool(be...  109 us
    pallas_call x1, Pallas kernels, chain_forward(): pl.pallas_call(functools.partial(fwd_kernel, heads, steps), grid_spec=plt...  66.6 us
    ppermute x31, waiting for transfers between devices, swap(): lax.ppermute(value, axis, [(source, source ^ mask) for source in range(co...  53.6 us
    ppermute x31, starting transfers between devices, swap(): lax.ppermute(value, axis, [(source, source ^ mask) for source in range(co...  29.7 us
    dot_general x8, matrix products, t_dot(): lax.dot_general(left, right, (((0,), (0,)), ((), ())), precision=high)  28.5 us
    dot_general x5, matrix products, dot_t(): lax.dot_general(left, right, (((1,), (1,)), ((), ())), precision=high)  24.9 us
    dot_general x4, matrix products, dot(): return jnp.dot(left, right, precision=high)  21.3 us
    unnamed x180, local copies, waits for them, and re-layouts  20.1 us
  transfers between devices with their start and end apart: 33, of which 17 were waited for; matrix products, arithmetic and copies ran while one was open for 23% of the time, Pallas kernels for 23%

profile of v1, /device:TPU:0, one launch (start us, length us, event | category | flops | bytes accessed | tf_op | source)
XLA Modules:
  0.0 484.9 jit_solution(12191693647814071459)
XLA Ops:
  2.1 2.1 fusion.26
  4.3 3.0 collective-permute-start
  12.6 3.0 copy-done.7
  15.6 1.7 copy-done.8
  19.8 1.7 bitcast_subtract_fusion
  21.5 3.6 collective-permute-done
  28.6 2.4 fusion.57
  34.7 2.4 fusion.62.gate_ref
  37.7 9.2 %fusion.61.qkv_ref = f32[1024,640]{1,0:T(8,128)} fusion(f32[1024,768]{1,0:T(8,128)S(1)} %bitcast.277, f32[768,640]{1,0:T(8,128)S(1)} %copy-done.3), kind=kOutput, calls=%fused_computation.217 | convolution fusion | flops 6039797760 | bytes 7733248 | tf_op jit(solution)/shard_map/dot_general | solution.py:893
  46.9 66.6 %shard_map.306 = (f32[1024,256]{1,0:T(8,128)}, f32[1024,256]{1,0:T(8,128)}, bf16[64,3,128,256]{3,2,1,0:T(8,128)(2,1)}, bf16[64,3,128,256]{3,2,1,0:T(8,128)(2,1)}...) custom-call(s32[64]{0:T(128)} %convert_element_type.11.resets_ref, ...), custom_call_target="tpu_custom_call" | custom-call | flops 96000000000 | bytes 1048576 | tf_op jit(solution)/shard_map/pallas_call | solution.py:645
  113.5 2.4 copy.162
  115.9 3.5 all-to-all-start
  119.4 2.3 pad_maximum_fusion.14
  121.8 6.8 %fusion.48 = f32[256,2048]{1,0:T(8,128)} fusion(f32[2048,768]{1,0:T(8,128)} %param.35, f32[1,256,768]{2,1,0:T(8,128)S(1)} %copy-done.41), kind=kOutput, calls=%fused_computation.205 | convolution fusion | flops 2415919104 | bytes 9175040 | tf_op jit(solution)/shard_map/dot_general | solution.py:701
  128.5 2.5 all-to-all-done
  131.9 2.7 multiply_reduce_fusion.5
  135.7 9.5 %fusion.63 = f32[256,4096]{1,0:T(8,128)S(1)} fusion(f32[256,768]{1,0:T(8,128)} %multiply_multiply_fusion.1, f32[768,4096]{1,0:T(8,128)} %param.34), kind=kOutput, calls=%fused_computation.219 | convolution fusion | flops 4831838208 | bytes 17563648 | tf_op jit(solution)/shard_map/dot_general | solution.py:697
  145.2 4.1 add_multiply_fusion
  149.4 3.5 fusion.30
  152.9 8.8 %multiply_reduce_fusion.2 = (f32[768]{0:T(1024)S(1)}, f32[256]{0:T(256)S(1)}, f32[256,768]{1,0:T(8,128)}) fusion(f32[256,768]{1,0:T(8,128)S(1)} %get-tuple-element.215, f32[256]{0:T(256)S(1)} %add_rsqrt_fusion, f32[768]{0:T(1024)S(1)} %copy-done.68, f32[768,4096]{1,0:T(8,128)S(1)} %bitcast.282, f32[256,2048]{1,0:T(8,128)} %get-tuple-element.369, ...), kind=kOutput, calls=%fused_computation.88 | convolution fusion | flops 4834065408 | bytes 18358272 | tf_op jit(solution)/shard_map/dot_general | solution.py:701
  161.7 2.4 fusion.15
  167.9 1.8 fusion.33
  170.6 2.2 fusion.64
  172.8 3.5 all-to-all-start.1
  177.0 3.1 maximum_bitcast_fusion
  181.1 17.3 %all-to-all-done.1 = f32[4,256,192]{1,2,0:T(8,128)S(1)} async-done(((f32[4,256,192]{1,2,0:T(8,128)}), f32[4,256,192]{1,2,0:T(8,128)S(1)}, u32[]{:S(2)}, u32[]{:S(2)}) %all-to-all-start.1) | async-done | bytes 786464 | tf_op jit(solution)/shard_map/all_to_all | solution.py:801
  198.7 3.1 fusion.50
  201.9 2.2 convolution_add_fusion.2
  205.0 4.8 broadcast_select_fusion
  211.8 1.7 collective-permute-start.6
  213.5 3.9 convolution_add_fusion
  219.4 39.9 %shard_map.307 = (f32[384,640]{1,0:T(8,128)}, f32[3,64,256]{2,1,0:T(8,128)}, f32[3,16,256]{2,1,0:T(8,128)}, f32[3,64,256]{2,1,0:T(8,128)}, f32[3,16,128]{2,1,0:T...) custom-call(s32[64]{0:T(128)} %convert_element_type.11.resets_ref, ...), custom_call_target="tpu_custom_call" | custom-call | flops 48000000000 | bytes 1048576 | tf_op jit(solution)/shard_map/pallas_call | solution.py:674
  262.3 3.1 fusion.24
  265.5 2.7 multiply_reduce_fusion.3
  268.3 1.9 bitcast_add_fusion.2
  270.7 7.6 %fusion.7 = f32[768,1024]{1,0:T(8,128)S(1)} fusion(f32[1,2,256,1024]{3,2,1,0:T(8,128)} %bitcast.33, f32[1,2,256,1024]{3,2,1,0:T(8,128)S(1)} %copy-done.60, f32[2,1,256,768]{3,2,0,1:T(8,128)} %bitcast.32, f32[2,1,256,768]{3,2,0,1:T(8,128)S(1)} %copy-done.61), kind=kOutput, calls=%fused_computation.36 | convolution fusion | flops 4833673216 | bytes 10485760 | tf_op jit(solution)/shard_map/dot_general | solution.py:705
  278.9 1.7 select_bitcast_fusion.1
  281.9 1.7 collective-permute-start.11
  285.2 40.6 %shard_map.308 = (f32[384,640]{1,0:T(8,128)}, f32[3,64,256]{2,1,0:T(8,128)}, f32[3,16,256]{2,1,0:T(8,128)}, f32[3,64,256]{2,1,0:T(8,128)}, f32[3,16,128]{2,1,0:T...) custom-call(s32[64]{0:T(128)} %convert_element_type.11.resets_ref, ...), custom_call_target="tpu_custom_call" | custom-call | flops 48000000000 | bytes 1048576 | tf_op jit(solution)/shard_map/pallas_call | solution.py:674
  325.8 6.8 %fusion.12 = f32[1,256,768]{2,1,0:T(8,128)} fusion(f32[256,768]{1,0:T(8,128)S(1)} %copy-done.15, f32[256,2048]{1,0:T(8,128)S(1)} %copy-done.13, f32[2048,768]{1,0:T(8,128)} %param.35), kind=kOutput, calls=%fused_computation.51 | convolution fusion | flops 2416115712 | bytes 9961472 | tf_op jit(solution)/shard_map/dot_general | solution.py:697
  334.5 2.3 bitcast_add_fusion
  337.6 2.6 collective-permute-start.12
  340.2 28.5 %shard_map.309 = (f32[256,640]{1,0:T(8,128)}, f32[3,64,256]{2,1,0:T(8,128)}, f32[3,16,256]{2,1,0:T(8,128)}, f32[3,64,256]{2,1,0:T(8,128)}, f32[3,16,128]{2,1,0:T...) custom-call(s32[64]{0:T(128)} %convert_element_type.11.resets_ref, ...), custom_call_target="tpu_custom_call" | custom-call | flops 32000000000 | bytes 1048576 | tf_op jit(solution)/shard_map/pallas_call | solution.py:674
  369.0 2.1 collective-permute-done.13
  373.1 1.7 collective-permute-start.30
  378.5 4.5 fusion.65
  387.8 4.0 convolution_add_fusion.1
  397.2 1.9 multiply_reduce_fusion
  399.6 2.2 fusion.28
  402.9 1.7 pad_maximum_fusion.16
  407.4 1.7 copy.192
  409.2 1.7 bitcast_add_fusion.5
  411.3 1.7 bitcast_add_fusion.1
  414.6 2.1 collective-permute-start.25
  416.7 5.5 %collective-permute-done.15 = f32[2,2,56,256]{3,2,1,0:T(8,128)S(1)} collective-permute-done((f32[2,2,56,256]{3,2,1,0:T(8,128)S(1)}, f32[2,2,56,256]{3,2,1,0:T(8,128)S(1)}, u32[]{:S(2)}, u32[]{:S(2)}) %collective-permute-start.15) | collective-permute-done | bytes 229408 | tf_op jit(solution)/shard_map/ppermute | solution.py:710
  422.2 2.0 collective-permute-start.16
  426.7 4.0 collective-permute-done.16
  430.8 2.3 collective-permute-start.17
  433.2 2.9 collective-permute-done.17
  436.2 2.1 collective-permute-start.18
  439.7 8.2 %collective-permute-done.18 = f32[56,256]{1,0:T(8,128)S(1)} collective-permute-done((f32[56,256]{1,0:T(8,128)S(1)}, f32[56,256]{1,0:T(8,128)S(1)}, u32[]{:S(2)}, u32[]{:S(2)}) %collective-permute-start.18) | collective-permute-done | bytes 57376 | tf_op jit(solution)/shard_map/ppermute | solution.py:710
  448.0 4.2 collective-permute-done.26
  455.7 6.1 %collective-permute-done.27 = f32[96,640]{1,0:T(8,128)S(1)} collective-permute-done((f32[96,640]{1,0:T(8,128)S(1)}, f32[96,640]{1,0:T(8,128)S(1)}, u32[]{:S(2)}, u32[]{:S(2)}) %collective-permute-start.27) | collective-permute-done | bytes 245792 | tf_op jit(solution)/shard_map/ppermute | solution.py:710
  463.3 11.8 %collective-permute-done.22 = f32[8,56,256]{2,1,0:T(8,128)S(1)} collective-permute-done((f32[8,56,256]{2,1,0:T(8,128)S(1)}, f32[8,56,256]{2,1,0:T(8,128)S(1)}, u32[]{:S(2)}, u32[]{:S(2)}) %collective-permute-start.22) | collective-permute-done | bytes 458784 | tf_op jit(solution)/shard_map/ppermute | solution.py:710
  (347 shorter events, 81.0 us)
Async XLA Ops:
  0.7 131.2 %copy-start = (f32[768,768]{1,0:T(8,128)S(1)}, f32[768,768]{1,0:T(8,128)}, u32[]{:S(2)}) copy-start(f32[768,768]{1,0:T(8,128)} %param.32) | copy-start | bytes 7077892
  0.7 6.6 %copy-start.76 = (f32[12,64]{1,0:T(8,128)S(1)}, f32[12,64]{1,0:T(8,128)}, u32[]{:S(2)}) copy-start(f32[12,64]{1,0:T(8,128)} %param.28) | copy-start | bytes 9220
  0.7 10.8 %copy-start.82 = (f32[12]{0:T(128)S(1)}, f32[12]{0:T(128)}, u32[]{:S(2)}) copy-start(f32[12]{0:T(128)} %param.24) | copy-start | bytes 148
  0.7 10.9 %copy-start.71 = (f32[768,12]{0,1:T(8,128)S(1)}, f32[768,12]{0,1:T(8,128)}, u32[]{:S(2)}) copy-start(f32[768,12]{0,1:T(8,128)} %param.23) | copy-start | bytes 110596
  0.7 11.1 %copy-start.83 = (s32[1,4]{1,0:T(1,128)S(1)}, s32[1,4]{1,0:T(1,128)}, u32[]{:S(2)}) copy-start(s32[1,4]{1,0:T(1,128)} %param.19) | copy-start | bytes 52
  2.1 23.0 %copy-start.72 = (f32[256]{0:T(256)}, f32[256]{0:T(256)S(1)}, u32[]{:S(2)}) copy-start(f32[256]{0:T(256)S(1)} %add_rsqrt_fusion.1) | copy-start | bytes 3076
  4.3 20.8 %collective-permute-start = (f32[256,768]{1,0:T(8,128)}, f32[256,768]{1,0:T(8,128)}, u32[]{:S(2)}, u32[]{:S(2)}) collective-permute-start(f32[256,768]{1,0:T(8,128)} %fusion.26), channel_id=1, source_target_pairs={{0,2},{1,3},{2,0},{3,1},{4,6},{5,7},{6,4},{7,5},{8,10},{9,11},{10,... | collective-permute-start | bytes 2359304 | tf_op jit(solution)/shard_map/ppermute | solution.py:710
  17.3 7.9 %copy-start.18 = (f32[1,256,768]{2,1,0:T(8,128)S(1)}, f32[1,256,768]{2,1,0:T(8,128)}, u32[]{:S(2)}) copy-start(f32[1,256,768]{2,1,0:T(8,128)} %param.18) | copy-start | bytes 2359300
  17.3 7.9 %copy-start.69 = (f32[768]{0:T(1024)S(1)}, f32[768]{0:T(1024)}, u32[]{:S(2)}) copy-start(f32[768]{0:T(1024)} %param.21) | copy-start | bytes 9220
  18.4 10.2 %copy-start.2 = (f32[768,640]{1,0:T(8,128)}, f32[768,640]{1,0:T(8,128)S(1)}, u32[]{:S(2)}) copy-start(f32[768,640]{1,0:T(8,128)S(1)} %get-tuple-element.153) | copy-start | bytes 5898244
  18.4 16.3 %copy-start.5 = (f32[768,256]{1,0:T(8,128)}, f32[768,256]{1,0:T(8,128)S(1)}, u32[]{:S(2)}) copy-start(f32[768,256]{1,0:T(8,128)S(1)} %get-tuple-element.155) | copy-start | bytes 2359300
  28.6 3.8 collective-permute-start.1
  115.9 15.1 %all-to-all-start = ((f32[4,256,192]{1,2,0:T(8,128)}), f32[4,256,192]{1,2,0:T(8,128)S(1)}, u32[]{:S(2)}, u32[]{:S(2)}) async-start(f32[4,256,192]{1,2,0:T(8,128)} %copy.162), calls=%async_computation | async-start | bytes 1572864 | tf_op jit(solution)/shard_map/all_to_all | solution.py:794
  134.6 45.5 %copy-start.14 = (f32[256,768]{1,0:T(8,128)}, f32[256,768]{1,0:T(8,128)S(1)}, u32[]{:S(2)}) copy-start(f32[256,768]{1,0:T(8,128)S(1)} %get-tuple-element.215) | copy-start | bytes 2359300
  135.7 17.1 %slice-start = ((s8[12582912]{0:T(1024)(128)(4,1)}), s8[4194304]{0:T(1024)(128)(4,1)S(1)}, s32[]{:S(2)}) async-start(s8[12582912]{0:T(1024)(128)(4,1)} %bitcast.281), calls=%async_computation.2 | async-start | bytes 8388608
  135.7 17.2 %slice-start.1 = ((s8[12582912]{0:T(1024)(128)(4,1)}), s8[4194304]{0:T(1024)(128)(4,1)S(1)}, s32[]{:S(2)}) async-start(s8[12582912]{0:T(1024)(128)(4,1)} %bitcast.281), calls=%async_computation.3 | async-start | bytes 8388608
  145.2 7.7 %slice-start.2 = ((s8[12582912]{0:T(1024)(128)(4,1)}), s8[4194304]{0:T(1024)(128)(4,1)S(1)}, s32[]{:S(2)}) async-start(s8[12582912]{0:T(1024)(128)(4,1)} %bitcast.281), calls=%async_computation.4 | async-start | bytes 8388608
  152.9 60.6 %collective-permute-start.4 = (f32[2048,384]{1,0:T(8,128)}, f32[2048,384]{1,0:T(8,128)}, u32[]{:S(2)}, u32[]{:S(2)}) collective-permute-start(f32[2048,384]{1,0:T(8,128)} %fusion.30), channel_id=1, source_target_pairs={{0,1},{1,0},{2,3},{3,2},{4,5},{5,4},{6,7},{7,6},{8,9},{9,8},{10,11... | collective-permute-start | bytes 9437192 | tf_op jit(solution)/shard_map/ppermute | solution.py:710
  152.9 8.8 %copy-start.20 = (f32[256,2048]{1,0:T(8,128)S(1)}, f32[256,2048]{1,0:T(8,128)}, u32[]{:S(2)}) copy-start(f32[256,2048]{1,0:T(8,128)} %get-tuple-element.369) | copy-start | bytes 6291460
  165.6 39.4 %collective-permute-start.3 = (f32[2,256,1024]{2,1,0:T(8,128)}, f32[2,256,1024]{2,1,0:T(8,128)}, u32[]{:S(2)}, u32[]{:S(2)}) collective-permute-start(f32[2,256,1024]{2,1,0:T(8,128)} %pad_maximum_fusion.6), channel_id=1, source_target_pairs={{0,1},{1,0},{2,3},{3,2},{4,5},{5,4},{6,7},{7,6},{8,9},{9,8},{10,11... | collective-permute-start | bytes 6291464 | tf_op jit(solution)/shard_map/ppermute | solution.py:710
  169.7 32.1 %collective-permute-start.2 = (f32[768,384]{1,0:T(8,128)}, f32[768,384]{1,0:T(8,128)}, u32[]{:S(2)}, u32[]{:S(2)}) collective-permute-start(f32[768,384]{1,0:T(8,128)} %fusion.33), channel_id=1, source_target_pairs={{0,1},{1,0},{2,3},{3,2},{4,5},{5,4},{6,7},{7,6},{8,9},{9,8},{10,11... | collective-permute-start | bytes 3538952 | tf_op jit(solution)/shard_map/ppermute | solution.py:710
  170.2 28.4 %collective-permute-start.8 = (f32[256,768]{1,0:T(8,128)}, f32[256,768]{1,0:T(8,128)}, u32[]{:S(2)}, u32[]{:S(2)}) collective-permute-start(f32[256,768]{1,0:T(8,128)} %multiply_multiply_fusion.1), channel_id=1, source_target_pairs={{0,2},{1,3},{2,0},{3,1},{4,6},{5,7},{6,4},{7,5},{8,10},{9,11},{10,... | collective-permute-start | bytes 2359304 | tf_op jit(solution)/shard_map/ppermute | solution.py:710
  172.8 25.5 %all-to-all-start.1 = ((f32[4,256,192]{1,2,0:T(8,128)}), f32[4,256,192]{1,2,0:T(8,128)S(1)}, u32[]{:S(2)}, u32[]{:S(2)}) async-start(f32[4,256,192]{1,2,0:T(8,128)} %bitcast.301), calls=%async_computation.1 | async-start | bytes 1572864 | tf_op jit(solution)/shard_map/all_to_all | solution.py:801
  181.1 17.6 %copy-start.59 = (f32[1,256,768]{2,1,0:T(8,128)S(1)}, f32[1,256,768]{2,1,0:T(8,128)}, u32[]{:S(2)}) copy-start(f32[1,256,768]{2,1,0:T(8,128)} %fusion.92) | copy-start | bytes 2359300
  201.9 68.3 %collective-permute-start.9 = (f32[2,256,768]{2,1,0:T(8,128)}, f32[2,256,768]{2,1,0:T(8,128)}, u32[]{:S(2)}, u32[]{:S(2)}) collective-permute-start(f32[2,256,768]{2,1,0:T(8,128)} %get-tuple-element.394), channel_id=1, source_target_pairs={{0,1},{1,0},{2,3},{3,2},{4,5},{5,4},{6,7},{7,6},{8,9},{9,8},{10,11... | collective-permute-start | bytes 4718600 | tf_op jit(solution)/shard_map/ppermute | solution.py:710
  205.0 4.8 copy-start.62
  211.4 48.2 %collective-permute-start.7 = (f32[2,256,1024]{2,1,0:T(8,128)}, f32[2,256,1024]{2,1,0:T(8,128)}, u32[]{:S(2)}, u32[]{:S(2)}) collective-permute-start(f32[2,256,1024]{2,1,0:T(8,128)} %get-tuple-element.188), channel_id=1, source_target_pairs={{0,2},{1,3},{2,0},{3,1},{4,6},{5,7},{6,4},{7,5},{8,10},{9,11},{10,... | collective-permute-start | bytes 6291464 | tf_op jit(solution)/shard_map/ppermute | solution.py:710
  211.8 47.5 %collective-permute-start.6 = (f32[2,2,96,384]{3,2,1,0:T(8,128)}, f32[2,2,96,384]{3,2,1,0:T(8,128)}, u32[]{:S(2)}, u32[]{:S(2)}) collective-permute-start(f32[2,2,96,384]{3,2,1,0:T(8,128)} %select_bitcast_fusion.14), channel_id=1, source_target_pairs={{0,4},{4,0},{8,12},{12,8},{16,20},{20,16},{24,28},{28,24},{1,5},{5... | collective-permute-start | bytes 1769480 | tf_op jit(solution)/shard_map/ppermute | solution.py:710
  218.8 42.3 %collective-permute-start.5 = (f32[2,2,256,384]{3,2,0,1:T(8,128)S(1)}, f32[2,2,256,384]{3,2,0,1:T(8,128)}, u32[]{:S(2)}, u32[]{:S(2)}) collective-permute-start(f32[2,2,256,384]{3,2,0,1:T(8,128)S(1)} %select_bitcast_fusion.3), channel_id=1, source_target_pairs={{0,4},{4,0},{8,12},{12,8},{16,20},{20,16},{24,28},{28,24},{1,5},{5... | collective-permute-start | bytes 4718600 | tf_op jit(solution)/shard_map/ppermute | solution.py:710
  262.3 18.3 %copy-start.50 = (f32[2,2,96,384]{3,2,1,0:T(8,128)}, f32[2,2,96,384]{3,2,1,0:T(8,128)S(1)}, u32[]{:S(2)}) copy-start(f32[2,2,96,384]{3,2,1,0:T(8,128)S(1)} %bitcast_add_fusion.7) | copy-start | bytes 1769476
  270.2 10.5 %copy-start.29 = (f32[2,2,256,384]{3,2,0,1:T(8,128)}, f32[2,2,256,384]{3,2,0,1:T(8,128)S(1)}, u32[]{:S(2)}) copy-start(f32[2,2,256,384]{3,2,0,1:T(8,128)S(1)} %bitcast_add_fusion.2) | copy-start | bytes 4718596
  281.9 43.9 %copy-start.15 = (f32[256,768]{1,0:T(8,128)S(1)}, f32[256,768]{1,0:T(8,128)}, u32[]{:S(2)}) copy-start(f32[256,768]{1,0:T(8,128)} %copy-done.14) | copy-start | bytes 2359300
  281.9 50.7 %collective-permute-start.11 = (f32[2,2,96,1216]{3,2,0,1:T(8,128)}, f32[2,2,96,1216]{3,2,0,1:T(8,128)}, u32[]{:S(2)}, u32[]{:S(2)}) collective-permute-start(f32[2,2,96,1216]{3,2,0,1:T(8,128)} %select_bitcast_fusion.1), channel_id=1, source_target_pairs={{0,4},{4,0},{8,12},{12,8},{16,20},{20,16},{24,28},{28,24},{1,5},{5... | collective-permute-start | bytes 5603336 | tf_op jit(solution)/shard_map/ppermute | solution.py:710
  283.6 49.0 %collective-permute-start.10 = (f32[2,352,384]{2,1,0:T(8,128)}, f32[2,352,384]{2,1,0:T(8,128)}, u32[]{:S(2)}, u32[]{:S(2)}) collective-permute-start(f32[2,352,384]{2,1,0:T(8,128)} %select_bitcast_fusion.6), channel_id=1, source_target_pairs={{0,8},{4,12},{8,0},{12,4},{16,24},{20,28},{24,16},{28,20},{1,9},{5... | collective-permute-start | bytes 3244040 | tf_op jit(solution)/shard_map/ppermute | solution.py:710
  325.8 6.8 %copy-start.30 = (f32[2,2,256,384]{3,2,0,1:T(8,128)S(1)}, f32[2,2,256,384]{3,2,0,1:T(8,128)}, u32[]{:S(2)}) copy-start(f32[2,2,256,384]{3,2,0,1:T(8,128)} %copy-done.29) | copy-start | bytes 4718596
  325.8 6.8 %copy-start.51 = (f32[2,2,96,384]{3,2,1,0:T(8,128)S(1)}, f32[2,2,96,384]{3,2,1,0:T(8,128)}, u32[]{:S(2)}) copy-start(f32[2,2,96,384]{3,2,1,0:T(8,128)} %copy-done.50) | copy-start | bytes 1769476
  337.0 34.1 %copy-start.36 = (f32[2,352,384]{2,1,0:T(8,128)S(1)}, f32[2,352,384]{2,1,0:T(8,128)}, u32[]{:S(2)}) copy-start(f32[2,352,384]{2,1,0:T(8,128)} %copy-done.35) | copy-start | bytes 3244036
  337.0 34.1 %collective-permute-start.13 = (f32[2,96,1216]{2,1,0:T(8,128)S(1)}, f32[2,96,1216]{2,1,0:T(8,128)}, u32[]{:S(2)}, u32[]{:S(2)}) collective-permute-start(f32[2,96,1216]{2,1,0:T(8,128)S(1)} %select_bitcast_fusion.8), channel_id=1, source_target_pairs={{0,8},{4,12},{8,0},{12,4},{16,24},{20,28},{24,16},{28,20},{1,9},{5... | collective-permute-start | bytes 2801672 | tf_op jit(solution)/shard_map/ppermute | solution.py:710
  337.6 31.4 %collective-permute-start.12 = (f32[352,384]{1,0:T(8,128)S(1)}, f32[352,384]{1,0:T(8,128)}, u32[]{:S(2)}, u32[]{:S(2)}) collective-permute-start(f32[352,384]{1,0:T(8,128)S(1)} %select_bitcast_fusion.15), channel_id=1, source_target_pairs={{0,16},{4,20},{8,24},{12,28},{16,0},{20,4},{24,8},{28,12},{1,17},{... | collective-permute-start | bytes 1622024 | tf_op jit(solution)/shard_map/ppermute | solution.py:710
  373.1 5.3 %copy-start.65 = (f32[256,640]{1,0:T(8,128)S(1)}, f32[256,640]{1,0:T(8,128)}, u32[]{:S(2)}) copy-start(f32[256,640]{1,0:T(8,128)} %get-tuple-element.261) | copy-start | bytes 1966084
  373.1 31.6 %collective-permute-start.30 = (f32[352,192]{1,0:T(8,128)S(1)}, f32[352,192]{1,0:T(8,128)}, u32[]{:S(2)}, u32[]{:S(2)}) collective-permute-start(f32[352,192]{1,0:T(8,128)S(1)} %slice_select_fusion), channel_id=1, source_target_pairs={{0,2},{1,3},{2,0},{3,1},{4,6},{5,7},{6,4},{7,5},{8,10},{9,11},{10,... | collective-permute-start | bytes 811016 | tf_op jit(solution)/shard_map/ppermute | solution.py:710
  376.9 47.3 %collective-permute-start.29 = (f32[96,1216]{1,0:T(8,128)}, f32[96,1216]{1,0:T(8,128)}, u32[]{:S(2)}, u32[]{:S(2)}) collective-permute-start(f32[96,1216]{1,0:T(8,128)} %select_bitcast_fusion.16), channel_id=1, source_target_pairs={{0,16},{4,20},{8,24},{12,28},{16,0},{20,4},{24,8},{28,12},{1,17},{... | collective-permute-start | bytes 1400840 | tf_op jit(solution)/shard_map/ppermute | solution.py:710
  378.5 7.7 %copy-start.21 = (f32[1024,640]{1,0:T(8,128)}, f32[1024,640]{1,0:T(8,128)S(1)}, u32[]{:S(2)}) copy-start(f32[1024,640]{1,0:T(8,128)S(1)} %constant_dynamic-update-slice_fusion) | copy-start | bytes 7864324
  385.5 23.6 %collective-permute-start.24 = (f32[2,2,96,640]{3,2,0,1:T(8,128)}, f32[2,2,96,640]{3,2,0,1:T(8,128)}, u32[]{:S(2)}, u32[]{:S(2)}) collective-permute-start(f32[2,2,96,640]{3,2,0,1:T(8,128)} %select_bitcast_fusion.7), channel_id=1, source_target_pairs={{0,4},{4,0},{8,12},{12,8},{16,20},{20,16},{24,28},{28,24},{1,5},{5... | collective-permute-start | bytes 2949128 | tf_op jit(solution)/shard_map/ppermute | solution.py:710
  393.9 5.2 %copy-start.70 = (f32[768]{0:T(1024)S(1)}, f32[768]{0:T(1024)}, u32[]{:S(2)}) copy-start(f32[768]{0:T(1024)} %param.21) | copy-start | bytes 9220
  393.9 5.3 %copy-start.77 = (f32[1,768]{1,0:T(1,128)S(1)}, f32[1,768]{1,0:T(1,128)}, u32[]{:S(2)}) copy-start(f32[1,768]{1,0:T(1,128)} %stack.166) | copy-start | bytes 9220
  393.9 16.9 %collective-permute-start.14 = (f32[2,256,768]{2,1,0:T(8,128)}, f32[2,256,768]{2,1,0:T(8,128)}, u32[]{:S(2)}, u32[]{:S(2)}) collective-permute-start(f32[2,256,768]{2,1,0:T(8,128)} %select_bitcast_fusion.2), channel_id=1, source_target_pairs={{0,1},{1,0},{2,3},{3,2},{4,5},{5,4},{6,7},{7,6},{8,9},{9,8},{10,11... | collective-permute-start | bytes 4718600 | tf_op jit(solution)/shard_map/ppermute | solution.py:710
  401.9 7.3 %copy-start.38 = (f32[2,2,1,96,640]{4,3,2,1,0:T(8,128)S(1)}, f32[2,2,1,96,640]{4,3,2,1,0:T(8,128)}, u32[]{:S(2)}) copy-start(f32[2,2,1,96,640]{4,3,2,1,0:T(8,128)} %copy-done.37) | copy-start | bytes 2949124
  401.9 7.3 %copy-start.40 = (f32[2,2,1,96,640]{4,3,2,1,0:T(8,128)S(1)}, f32[2,2,1,96,640]{4,3,2,1,0:T(8,128)}, u32[]{:S(2)}) copy-start(f32[2,2,1,96,640]{4,3,2,1,0:T(8,128)} %copy-done.39) | copy-start | bytes 2949124
  414.1 8.1 %collective-permute-start.15 = (f32[2,2,56,256]{3,2,1,0:T(8,128)S(1)}, f32[2,2,56,256]{3,2,1,0:T(8,128)S(1)}, u32[]{:S(2)}, u32[]{:S(2)}) collective-permute-start(f32[2,2,56,256]{3,2,1,0:T(8,128)S(1)} %select_bitcast_fusion.27), channel_id=1, source_target_pairs={{0,4},{4,0},{8,12},{12,8},{16,20},{20,16},{24,28},{28,24},{1,5},{5... | collective-permute-start | bytes 688136 | tf_op jit(solution)/shard_map/ppermute | solution.py:710
  414.6 18.6 %collective-permute-start.25 = (f32[2,96,640]{2,1,0:T(8,128)S(1)}, f32[2,96,640]{2,1,0:T(8,128)S(1)}, u32[]{:S(2)}, u32[]{:S(2)}) collective-permute-start(f32[2,96,640]{2,1,0:T(8,128)S(1)} %select_bitcast_fusion.19), channel_id=1, source_target_pairs={{0,8},{4,12},{8,0},{12,4},{16,24},{20,28},{24,16},{28,20},{1,9},{5... | collective-permute-start | bytes 1474568 | tf_op jit(solution)/shard_map/ppermute | solution.py:710
  422.2 8.5 %collective-permute-start.16 = (f32[2,56,256]{2,1,0:T(8,128)S(1)}, f32[2,56,256]{2,1,0:T(8,128)S(1)}, u32[]{:S(2)}, u32[]{:S(2)}) collective-permute-start(f32[2,56,256]{2,1,0:T(8,128)S(1)} %select_bitcast_fusion.30), channel_id=1, source_target_pairs={{0,8},{4,12},{8,0},{12,4},{16,24},{20,28},{24,16},{28,20},{1,9},{5... | collective-permute-start | bytes 344072 | tf_op jit(solution)/shard_map/ppermute | solution.py:710
  430.8 5.4 %collective-permute-start.17 = (f32[56,256]{1,0:T(8,128)S(1)}, f32[56,256]{1,0:T(8,128)S(1)}, u32[]{:S(2)}, u32[]{:S(2)}) collective-permute-start(f32[56,256]{1,0:T(8,128)S(1)} %select_bitcast_fusion.33), channel_id=1, source_target_pairs={{0,16},{4,20},{8,24},{12,28},{16,0},{20,4},{24,8},{28,12},{1,17},{... | collective-permute-start | bytes 172040 | tf_op jit(solution)/shard_map/ppermute | solution.py:710
  436.2 11.7 %collective-permute-start.18 = (f32[56,256]{1,0:T(8,128)S(1)}, f32[56,256]{1,0:T(8,128)S(1)}, u32[]{:S(2)}, u32[]{:S(2)}) collective-permute-start(f32[56,256]{1,0:T(8,128)S(1)} %bitcast_add_fusion.12), channel_id=1, source_target_pairs={{0,16},{4,20},{8,24},{12,28},{16,0},{20,4},{24,8},{28,12},{1,17},{... | collective-permute-start | bytes 172040 | tf_op jit(solution)/shard_map/ppermute | solution.py:710
  438.3 13.8 %collective-permute-start.26 = (f32[96,640]{1,0:T(8,128)S(1)}, f32[96,640]{1,0:T(8,128)S(1)}, u32[]{:S(2)}, u32[]{:S(2)}) collective-permute-start(f32[96,640]{1,0:T(8,128)S(1)} %select_bitcast_fusion.24), channel_id=1, source_target_pairs={{0,16},{4,20},{8,24},{12,28},{16,0},{20,4},{24,8},{28,12},{1,17},{... | collective-permute-start | bytes 737288 | tf_op jit(solution)/shard_map/ppermute | solution.py:710
  439.3 22.8 %collective-permute-start.21 = (f32[256,768]{1,0:T(8,128)S(1)}, f32[256,768]{1,0:T(8,128)S(1)}, u32[]{:S(2)}, u32[]{:S(2)}) collective-permute-start(f32[256,768]{1,0:T(8,128)S(1)} %select_bitcast_fusion.11), channel_id=1, source_target_pairs={{0,2},{1,3},{2,0},{3,1},{4,6},{5,7},{6,4},{7,5},{8,10},{9,11},{10,... | collective-permute-start | bytes 2359304 | tf_op jit(solution)/shard_map/ppermute | solution.py:710
  447.9 6.2 %collective-permute-start.19 = (f32[2,56,256]{2,1,0:T(8,128)S(1)}, f32[2,56,256]{2,1,0:T(8,128)S(1)}, u32[]{:S(2)}, u32[]{:S(2)}) collective-permute-start(f32[2,56,256]{2,1,0:T(8,128)S(1)} %pad_maximum_fusion.20), channel_id=1, source_target_pairs={{0,8},{4,12},{8,0},{12,4},{16,24},{20,28},{24,16},{28,20},{1,9},{5... | collective-permute-start | bytes 344072 | tf_op jit(solution)/shard_map/ppermute | solution.py:710
  452.2 9.6 %collective-permute-start.27 = (f32[96,640]{1,0:T(8,128)S(1)}, f32[96,640]{1,0:T(8,128)S(1)}, u32[]{:S(2)}, u32[]{:S(2)}) collective-permute-start(f32[96,640]{1,0:T(8,128)S(1)} %bitcast_add_fusion.11), channel_id=1, source_target_pairs={{0,2},{1,3},{2,0},{3,1},{4,6},{5,7},{6,4},{7,5},{8,10},{9,11},{10,... | collective-permute-start | bytes 737288 | tf_op jit(solution)/shard_map/ppermute | solution.py:710
  454.1 7.8 %collective-permute-start.20 = (f32[2,2,56,256]{3,2,0,1:T(8,128)S(1)}, f32[2,2,56,256]{3,2,0,1:T(8,128)S(1)}, u32[]{:S(2)}, u32[]{:S(2)}) collective-permute-start(f32[2,2,56,256]{3,2,0,1:T(8,128)S(1)} %pad_maximum_fusion.19), channel_id=1, source_target_pairs={{0,4},{4,0},{8,12},{12,8},{16,20},{20,16},{24,28},{28,24},{1,5},{5... | collective-permute-start | bytes 688136 | tf_op jit(solution)/shard_map/ppermute | solution.py:710
  461.9 14.5 %collective-permute-start.28 = (f32[2,96,640]{2,1,0:T(8,128)S(1)}, f32[2,96,640]{2,1,0:T(8,128)S(1)}, u32[]{:S(2)}, u32[]{:S(2)}) collective-permute-start(f32[2,96,640]{2,1,0:T(8,128)S(1)} %pad_maximum_fusion.15), channel_id=1, source_target_pairs={{0,1},{1,0},{2,3},{3,2},{4,5},{5,4},{6,7},{7,6},{8,9},{9,8},{10,11... | collective-permute-start | bytes 1474568 | tf_op jit(solution)/shard_map/ppermute | solution.py:710
  462.1 13.0 %collective-permute-start.22 = (f32[8,56,256]{2,1,0:T(8,128)S(1)}, f32[8,56,256]{2,1,0:T(8,128)S(1)}, u32[]{:S(2)}, u32[]{:S(2)}) collective-permute-start(f32[8,56,256]{2,1,0:T(8,128)S(1)} %bitcast.302), channel_id=1, source_target_pairs={{0,2},{1,3},{2,0},{3,1},{4,6},{5,7},{6,4},{7,5},{8,10},{9,11},{10,... | collective-permute-start | bytes 1376264 | tf_op jit(solution)/shard_map/ppermute | solution.py:710
  463.3 12.0 %copy-start.26 = (f32[256,768]{1,0:T(8,128)S(1)}, f32[256,768]{1,0:T(8,128)}, u32[]{:S(2)}) copy-start(f32[256,768]{1,0:T(8,128)} %copy-done.25) | copy-start | bytes 2359300
  475.2 2.5 collective-permute-start.23
  478.1 6.6 %copy-start.1 = (f32[768,768]{1,0:T(8,128)S(1)}, f32[768,768]{1,0:T(8,128)}, u32[]{:S(2)}) copy-start(f32[768,768]{1,0:T(8,128)} %param.32) | copy-start | bytes 7077892
  (56 other events, 140.4 us)
